TPU v7x, 32 devices: a whole 2x2x4 slice. The times are simulated.
32 devices in a mesh: lat: 8 (over z, y), lev: 4 (over x, core).
Axes of the slice: x: 2, y: 2, z: 4, core: 2. Of those that a mesh axis runs over, the one named last changes fastest.
Arguments:
- grid_old: bfloat16 [3, 4, 128, 5120], P(None, 'lev', 'lat'), may hold values from -6 to 6
- depart_offset: int32 [4, 128, 5120], P('lev', 'lat'), may hold values from -12 to 9, as said below
- interp_weights: bfloat16 [4, 4, 128, 5120], P(None, 'lev', 'lat'), may hold values from -0.25 to 0.75
- pair_order: int32 [384], replicated, may hold values from 0 to 383, each once
- legendre: bfloat16 [384, 769, 128], P(('lat', 'lev')), may hold values from -0.5 to 0.5
- helmholtz: float32 [768, 4, 4], replicated, may hold values from -3 to 3
Outputs:
- grid_new: bfloat16 [3, 4, 128, 5120], P(None, 'lev', 'lat')
Inputs may be any that keep to these rules, and one draw needn't show every extreme that they name: `depart_offset`: in the rows of each index of lat, every offset lies in -w to w - 3 for that band's width w, which is at most 12; some band has width 12 and reaches both ends. `pair_order`: A permutation of the wavenumber pairs.
All inputs are finite; a program needn't handle non-finite values.
Results may differ from a plain program's by a relative error of at most 0.017.
Values may be sent and summed in bfloat16 or wider, within the bound.
A program may use at most 64 MiB of HBM per device.

v0:
```python
import math

import jax
import jax.numpy as jnp
from jax import lax
from jax.sharding import PartitionSpec as P

HMAX = 12


def padded(block, sides, width):
    for axis, dim in sides:
        count = lax.axis_size(axis)
        forward = [(i, i + 1) for i in range(count - 1)]
        backward = [(target, source) for source, target in forward]
        low = lax.ppermute(
            lax.slice_in_dim(block, block.shape[dim] - width, None, axis=dim), axis, forward
        )
        high = lax.ppermute(lax.slice_in_dim(block, 0, width, axis=dim), axis, backward)
        block = jnp.concatenate([low, block, high], axis=dim)
    return block


def shards(grid_old, depart_offset, interp_weights, pair_order, legendre, helmholtz):
    lat_count = lax.axis_size("lat")
    lev_count = lax.axis_size("lev")
    fields, lev_local, row_count, lon_count = grid_old.shape
    pair_count = pair_order.shape[0]
    pair_local, slot_count, lat_total = legendre.shape
    wavenumber_count = helmholtz.shape[0]
    level_count = helmholtz.shape[1]
    column_count = 4 * fields * level_count
    local_columns = fields * lev_local * row_count
    extended = padded(grid_old, (("lat", 2),), HMAX)
    relative = depart_offset + HMAX
    weights_wide = [interp_weights[k].astype(jnp.float32) for k in range(4)]
    summed = jnp.zeros(grid_old.shape, jnp.float32)
    for shift_row in range(2 * HMAX + 1):
        coefficient = jnp.zeros(relative.shape, jnp.float32)
        for offset_term in range(4):
            coefficient = coefficient + jnp.where(
                relative + offset_term == shift_row, weights_wide[offset_term], 0.0
            )
        window = extended[:, :, shift_row : shift_row + row_count, :].astype(jnp.float32)
        summed = summed + coefficient[None] * window
    arrival = summed.astype(jnp.bfloat16)
    row_ident = jnp.arange(pair_count * 4, dtype=jnp.int32)
    slot_ident = row_ident // 4
    which_half = row_ident // 2 % 2
    component = row_ident % 2
    first_wave = jnp.take(pair_order, slot_ident, axis=0)
    row_wave = jnp.where(which_half == 0, first_wave, wavenumber_count - 1 - first_wave)
    longitude = jnp.arange(lon_count, dtype=jnp.int32)
    phase_index = row_wave[:, None] * longitude[None, :] % lon_count
    angle_value = phase_index.astype(jnp.float32) * (2.0 * math.pi / lon_count)
    norm_factor = 1.0 / math.sqrt(lon_count)
    basis_rows = (
        jnp.where(component[:, None] == 0, jnp.cos(angle_value), -jnp.sin(angle_value))
        * norm_factor
    ).astype(jnp.bfloat16)
    flat_grid = arrival.reshape(local_columns, lon_count)
    fourier = lax.dot_general(
        basis_rows, flat_grid, (((1,), (1,)), ((), ())), preferred_element_type=jnp.float32
    )
    fourier = fourier.astype(jnp.bfloat16)
    moved = lax.all_to_all(fourier, ("lat", "lev"), split_axis=0, concat_axis=1, tiled=True)
    moved = moved.reshape(pair_local, 2, 2, lat_count, lev_count, fields, lev_local, row_count)
    spectral_in = moved.transpose(0, 1, 2, 5, 4, 6, 3, 7)
    stacked = spectral_in.reshape(pair_local, column_count, lat_total)
    projected = jnp.einsum("ptj,pqj->pqt", legendre, stacked, preferred_element_type=jnp.float32)
    projected = projected.reshape(pair_local, 2, 2 * fields, level_count, slot_count)
    holder_index = lax.axis_index("lat") * lev_count + lax.axis_index("lev")
    slot_ids = holder_index * pair_local + jnp.arange(pair_local, dtype=jnp.int32)
    pair_here = jnp.take(pair_order, slot_ids, axis=0)
    coefficient_axis = jnp.arange(slot_count, dtype=jnp.int32)
    lower = coefficient_axis[None, :] < (wavenumber_count - pair_here)[:, None]
    lower_mask = lower[:, None, None, :]
    chosen = jnp.where(lower_mask, projected[:, 0], projected[:, 1])
    degree = jnp.where(
        lower, pair_here[:, None] + coefficient_axis[None, :], coefficient_axis[None, :] - 1
    )
    helm_table = helmholtz.reshape(wavenumber_count, level_count * level_count).T
    operator = jnp.take(helm_table, degree, axis=1).reshape(
        level_count, level_count, pair_local, slot_count
    )
    operator = operator.transpose(2, 0, 1, 3)
    solved_wide = jnp.zeros(chosen.shape, jnp.float32)
    for level_from in range(level_count):
        solved_wide = (
            solved_wide
            + operator[:, None, :, level_from, :] * chosen[:, :, level_from, :][:, :, None, :]
        )
    solved = solved_wide.astype(jnp.bfloat16)
    zero_part = jnp.zeros_like(solved)
    placed = jnp.stack(
        [jnp.where(lower_mask, solved, zero_part), jnp.where(lower_mask, zero_part, solved)], axis=1
    )
    placed = placed.reshape(pair_local, column_count, slot_count)
    returned = jnp.einsum("ptj,pqt->pqj", legendre, placed, preferred_element_type=jnp.float32)
    returned = returned.astype(jnp.bfloat16).reshape(
        pair_local, 2, 2, fields, lev_count, lev_local, lat_count, row_count
    )
    outgoing = returned.transpose(6, 4, 0, 1, 2, 3, 5, 7)
    outgoing = outgoing.reshape(lat_count * lev_count * pair_local * 4, local_columns)
    arrived = lax.all_to_all(outgoing, ("lat", "lev"), split_axis=0, concat_axis=0, tiled=True)
    wave_weight = jnp.where(row_wave == 0, 1.0, 2.0).astype(jnp.bfloat16)
    weighted = arrived * wave_weight[:, None]
    rebuilt = lax.dot_general(
        weighted, basis_rows, (((0,), (0,)), ((), ())), preferred_element_type=jnp.float32
    )
    return rebuilt.astype(jnp.bfloat16).reshape(fields, lev_local, row_count, lon_count)


def solution(mesh):
    in_specs = (
        P(None, "lev", "lat", None),
        P("lev", "lat", None),
        P(None, "lev", "lat", None),
        P(),
        P(("lat", "lev"), None, None),
        P(),
    )
    out_specs = P(None, "lev", "lat", None)
    return jax.shard_map(shards, mesh=mesh, in_specs=in_specs, out_specs=out_specs, check_vma=False)
```

profile of v0, /device:TPU:1, one launch (start us, length us, event | category | flops | bytes accessed | tf_op | source)
XLA Modules:
  0.0 416.0 jit_solution(10969105051810493339)
XLA Ops:
  0.0 2.4 fusion.150
  2.4 1.3 collective-permute-start.1
  3.7 5.4 %collective-permute-start = (bf16[3,1,12,5120]{3,2,1,0:T(8,128)(2,1)}, bf16[3,1,12,5120]{3,2,1,0:T(8,128)(2,1)}, u32[]{:S(2)}, u32[]{:S(2)}) collective-permute-start(bf16[3,1,12,5120]{3,2,1,0:T(8,128)(2,1)} %get-tuple-element.44), channel_id=1, source_target_pairs={{0,4},{4,8},{8,12},{12,16},{16,20},{20,24},{24,28},{1,5},{5,9},{9,... | collective-permute-start | bytes 1105928 | tf_op jit(solution)/shard_map/ppermute | solution.py:16
  9.1 2.9 fusion.25
  12.0 3.0 fusion.29
  15.0 3.0 fusion.33
  18.0 3.0 fusion.37
  21.0 3.0 fusion.89
  24.0 3.1 fusion.105
  27.0 0.8 constant_dynamic-update-slice_fusion.1
  27.9 0.9 fusion.121
  29.0 0.6 fusion.125
  29.6 0.7 gather_fusion
  30.3 0.7 fusion.124
  31.1 9.5 %gather_fusion.2 = s32[1536]{0:T(1024)S(1)} fusion(s32[384]{0:T(512)S(1)} %copy-done.1, s32[2048]{0:T(1024)S(1)} %pad_clamp_fusion.1), kind=kCustom, calls=%fused_computation.2 | custom fusion | bytes 18432 | tf_op jit(solution)/shard_map/jit(_take)/gather | solution.py:51
  40.6 0.6 select_convert_fusion
  41.5 18.1 %gather_fusion.1 = f32[9228,16]{1,0:T(8,128)} fusion(f32[16,768]{0,1:T(8,128)S(1)} %bitcast.225, s32[10240]{0:T(1024)S(1)} %pad_clamp_fusion), kind=kCustom, calls=%fused_computation.1 | custom fusion | bytes 1218096 | tf_op jit(solution)/shard_map/jit(_take)/gather | solution.py:83
  59.7 3.2 copy.21
  62.9 1.4 reshape.505
  64.3 135.4 %multiply_convert_fusion.11 = bf16[1536,5120]{1,0:T(8,128)(2,1)S(1)} fusion(s32[1536]{0:T(1024)} %get-tuple-element.6, pred[1536]{0:T(1024)(128)(4,1)} %fusion.125), kind=kLoop, calls=%fused_computation.6.clone.1.clone.clone.clone.1 | loop fusion | flops 102236160 | bytes 15736320 | tf_op jit(solution)/shard_map/dot_general | solution.py:62
  200.0 1.3 fusion.149
  201.3 1.1 constant_dynamic-update-slice_fusion
  202.4 10.6 %add_convert_fusion.1 = bf16[3,1,16,5120]{3,2,1,0:T(8,128)(2,1)} fusion(bf16[3,1,16,5120]{3,2,1,0:T(8,128)(2,1)} %param.6, bf16[3,1,12,5120]{3,2,1,0:T(8,128)(2,1)} %collective-permute-done, bf16[3,1,28,5120]{3,2,1,0:T(8,128)(2,1)S(1)} %constant_dynamic-update-slice_fusion, f32[16,5120]{1,0:T(8,128)} %fusion.121, f32[16,5120]{1,0:T(8,128)} %get-tuple-element.38, ...), kind=kLoop, calls=%fused_computation.144 | loop fusion | flops 27279360 | bytes 15441920 | tf_op jit(solution)/shard_map/convert_element_type | solution.py:46
  213.1 6.6 %fusion.8 = bf16[1536,48]{0,1:T(8,128)(2,1)} fusion(bf16[48,5120]{1,0:T(8,128)(2,1)} %bitcast.229, bf16[1536,5120]{1,0:T(8,128)(2,1)S(1)} %multiply_convert_fusion.11), kind=kOutput, calls=%fused_computation.114 | convolution fusion | flops 755048448 | bytes 16367616 | tf_op jit(solution)/shard_map/dot_general | solution.py:62
  219.7 1.1 copy.30
  220.8 1.2 reshape.518
  222.1 6.2 %all-to-all-start = ((bf16[32,2,1152]{2,1,0:T(2,128)(2,1)}), bf16[32,2,1152]{2,1,0:T(2,128)(2,1)}, u32[]{:S(2)}, u32[]{:S(2)}) async-start(bf16[32,2,1152]{2,1,0:T(2,128)(2,1)} %reshape.518), calls=%async_computation | async-start | bytes 294912 | tf_op jit(solution)/shard_map/all_to_all | solution.py:66
  228.3 0.8 copy_bitcast_fusion.5
  229.1 0.8 copy_bitcast_fusion.7
  229.9 6.8 %all-to-all-done = bf16[32,2,1152]{2,1,0:T(2,128)(2,1)} async-done(((bf16[32,2,1152]{2,1,0:T(2,128)(2,1)}), bf16[32,2,1152]{2,1,0:T(2,128)(2,1)}, u32[]{:S(2)}, u32[]{:S(2)}) %all-to-all-start) | async-done | bytes 147488 | tf_op jit(solution)/shard_map/all_to_all | solution.py:66
  236.8 1.3 reshape.519
  238.2 2.0 reshape.482
  240.2 2.8 copy.25
  243.0 2.1 reshape.483
  245.1 2.2 fusion.151
  247.3 2.9 reshape.484
  250.3 1.8 fusion.9
  252.1 0.7 fusion.148
  253.1 0.9 broadcast_select_fusion.1
  254.2 1.7 pad_maximum_fusion
  255.9 1.7 reshape.485
  257.6 1.3 convolution_convert_fusion
  258.9 2.6 reshape.486
  261.5 3.3 copy.52
  264.7 2.8 all_to_all.23
  267.6 0.6 reshape.520
  268.2 10.6 %all_to_all.28 = bf16[32,2,1152]{2,1,0:T(2,128)(2,1)S(1)} all-to-all(bf16[32,2,1152]{2,1,0:T(2,128)(2,1)S(1)} %reshape.520), channel_id=1, replica_groups=mesh['lat'=8,'lev'=4] {'lat','lev'}, dimensions={0} | all-to-all | bytes 294912 | tf_op jit(solution)/shard_map/all_to_all | solution.py:105
  279.4 136.1 %fusion.7 = bf16[48,5120]{1,0:T(8,128)(2,1)} fusion(bf16[1536,48]{1,0:T(8,128)(2,1)S(1)} %bitcast_multiply_fusion, s32[1536]{0:T(1024)S(1)} %copy-done.19, pred[1536]{0:T(1024)(128)(4,1)S(1)} %copy-done.20), kind=kOutput, calls=%fused_computation.13 | convolution fusion | flops 857456640 | bytes 646656 | tf_op jit(solution)/shard_map/dot_general | solution.py:108
  (62 shorter events, 2.2 us)
Async XLA Ops:
  0.0 245.1 %copy-start = (bf16[12,769,128]{2,1,0:T(8,128)(2,1)S(1)}, bf16[12,769,128]{2,1,0:T(8,128)(2,1)}, u32[]{:S(2)}) copy-start(bf16[12,769,128]{2,1,0:T(8,128)(2,1)} %param.10) | copy-start | bytes 7087108
  0.0 27.0 %copy-start.5 = (bf16[3,1,16,5120]{3,2,1,0:T(8,128)(2,1)S(1)}, bf16[3,1,16,5120]{3,2,1,0:T(8,128)(2,1)}, u32[]{:S(2)}) copy-start(bf16[3,1,16,5120]{3,2,1,0:T(8,128)(2,1)} %param.6) | copy-start | bytes 1474564
  0.0 27.9 %copy-start.4 = (s32[1,16,5120]{2,1,0:T(8,128)S(1)}, s32[1,16,5120]{2,1,0:T(8,128)}, u32[]{:S(2)}) copy-start(s32[1,16,5120]{2,1,0:T(8,128)} %param.7) | copy-start | bytes 983044
  0.0 27.9 %copy-start.3 = (bf16[4,1,16,5120]{3,2,1,0:T(8,128)(2,1)S(1)}, bf16[4,1,16,5120]{3,2,1,0:T(8,128)(2,1)}, u32[]{:S(2)}) copy-start(bf16[4,1,16,5120]{3,2,1,0:T(8,128)(2,1)} %param.8) | copy-start | bytes 1966084
  0.0 29.6 %copy-start.1 = (s32[384]{0:T(512)S(1)}, s32[384]{0:T(512)}, u32[]{:S(2)}) copy-start(s32[384]{0:T(512)} %param.9) | copy-start | bytes 4612
  0.0 41.3 %copy-start.17 = (f32[768,4,4]{0,2,1:T(4,128)S(1)}, f32[768,4,4]{0,2,1:T(4,128)}, u32[]{:S(2)}) copy-start(f32[768,4,4]{0,2,1:T(4,128)} %param.11) | copy-start | bytes 147460
  2.4 198.9 %collective-permute-start.1 = (bf16[3,1,12,5120]{3,2,1,0:T(8,128)(2,1)}, bf16[3,1,12,5120]{3,2,1,0:T(8,128)(2,1)}, u32[]{:S(2)}, u32[]{:S(2)}) collective-permute-start(bf16[3,1,12,5120]{3,2,1,0:T(8,128)(2,1)} %get-tuple-element.43), channel_id=1, source_target_pairs={{4,0},{8,4},{12,8},{16,12},{20,16},{24,20},{28,24},{5,1},{9,5},{13... | collective-permute-start | bytes 1105928 | tf_op jit(solution)/shard_map/ppermute | solution.py:19
  3.7 198.7 %collective-permute-start = (bf16[3,1,12,5120]{3,2,1,0:T(8,128)(2,1)}, bf16[3,1,12,5120]{3,2,1,0:T(8,128)(2,1)}, u32[]{:S(2)}, u32[]{:S(2)}) collective-permute-start(bf16[3,1,12,5120]{3,2,1,0:T(8,128)(2,1)} %get-tuple-element.44), channel_id=1, source_target_pairs={{0,4},{4,8},{8,12},{12,16},{16,20},{20,24},{24,28},{1,5},{5,9},{9,... | collective-permute-start | bytes 1105928 | tf_op jit(solution)/shard_map/ppermute | solution.py:16
  64.3 135.4 %copy-start.6 = (f32[12,769,16]{1,0,2:T(8,128)S(1)}, f32[12,769,16]{1,0,2:T(8,128)}, u32[]{:S(2)}) copy-start(f32[12,769,16]{1,0,2:T(8,128)} %reshape.505) | copy-start | bytes 1771780
  64.3 135.4 %copy-start.16 = (pred[12,769]{1,0:T(8,128)(4,1)S(1)}, pred[12,769]{1,0:T(8,128)(4,1)}, u32[]{:S(2)}) copy-start(pred[12,769]{1,0:T(8,128)(4,1)} %get-tuple-element.45) | copy-start | bytes 27688
  64.3 137.1 %copy-start.2 = (bf16[3,1,28,5120]{3,2,1,0:T(8,128)(2,1)S(1)}, bf16[3,1,28,5120]{3,2,1,0:T(8,128)(2,1)}, u32[]{:S(2)}) copy-start(bf16[3,1,28,5120]{3,2,1,0:T(8,128)(2,1)} %constant_dynamic-update-slice_fusion.1) | copy-start | bytes 2580484
  213.0 15.2 %copy-start.9 = (f32[12,4,1,769]{3,2,1,0:T(1,128)S(1)}, f32[12,4,1,769]{3,2,1,0:T(1,128)}, u32[]{:S(2)}) copy-start(f32[12,4,1,769]{3,2,1,0:T(1,128)} %get-tuple-element.40) | copy-start | bytes 442948
  213.0 15.2 %copy-start.10 = (f32[12,4,1,769]{3,2,1,0:T(1,128)S(1)}, f32[12,4,1,769]{3,2,1,0:T(1,128)}, u32[]{:S(2)}) copy-start(f32[12,4,1,769]{3,2,1,0:T(1,128)} %get-tuple-element.41) | copy-start | bytes 442948
  213.1 16.0 %copy-start.7 = (f32[12,4,1,769]{3,2,1,0:T(1,128)S(1)}, f32[12,4,1,769]{3,2,1,0:T(1,128)}, u32[]{:S(2)}) copy-start(f32[12,4,1,769]{3,2,1,0:T(1,128)} %get-tuple-element.39) | copy-start | bytes 442948
  213.1 16.0 %copy-start.8 = (f32[12,4,1,769]{3,2,1,0:T(1,128)S(1)}, f32[12,4,1,769]{3,2,1,0:T(1,128)}, u32[]{:S(2)}) copy-start(f32[12,4,1,769]{3,2,1,0:T(1,128)} %get-tuple-element.42) | copy-start | bytes 442948
  213.1 37.2 %copy-start.15 = (pred[12,769]{1,0:T(8,128)(4,1)S(1)}, pred[12,769]{1,0:T(8,128)(4,1)}, u32[]{:S(2)}) copy-start(pred[12,769]{1,0:T(8,128)(4,1)} %get-tuple-element.46) | copy-start | bytes 27688
  222.1 14.7 %all-to-all-start = ((bf16[32,2,1152]{2,1,0:T(2,128)(2,1)}), bf16[32,2,1152]{2,1,0:T(2,128)(2,1)}, u32[]{:S(2)}, u32[]{:S(2)}) async-start(bf16[32,2,1152]{2,1,0:T(2,128)(2,1)} %reshape.518), calls=%async_computation | async-start | bytes 294912 | tf_op jit(solution)/shard_map/all_to_all | solution.py:66
  229.1 23.9 %copy-start.11 = (f32[12,4,769]{2,1,0:T(4,128)S(1)}, f32[12,4,769]{2,1,0:T(4,128)}, u32[]{:S(2)}) copy-start(f32[12,4,769]{2,1,0:T(4,128)} %get-tuple-element.51) | copy-start | bytes 442948
  229.1 24.0 %copy-start.12 = (f32[12,4,769]{2,1,0:T(4,128)S(1)}, f32[12,4,769]{2,1,0:T(4,128)}, u32[]{:S(2)}) copy-start(f32[12,4,769]{2,1,0:T(4,128)} %get-tuple-element.52) | copy-start | bytes 442948
  238.2 14.9 %copy-start.13 = (f32[12,4,769]{2,1,0:T(4,128)S(1)}, f32[12,4,769]{2,1,0:T(4,128)}, u32[]{:S(2)}) copy-start(f32[12,4,769]{2,1,0:T(4,128)} %get-tuple-element.53) | copy-start | bytes 442948
  238.2 14.9 %copy-start.14 = (f32[12,4,769]{2,1,0:T(4,128)S(1)}, f32[12,4,769]{2,1,0:T(4,128)}, u32[]{:S(2)}) copy-start(f32[12,4,769]{2,1,0:T(4,128)} %get-tuple-element.54) | copy-start | bytes 442948
  247.3 31.8 %copy-start.18 = (bf16[1536]{0:T(1024)(128)(2,1)S(1)}, bf16[1536]{0:T(1024)(128)(2,1)}, u32[]{:S(2)}) copy-start(bf16[1536]{0:T(1024)(128)(2,1)} %get-tuple-element.5) | copy-start | bytes 9220
  247.3 32.1 %copy-start.19 = (s32[1536]{0:T(1024)S(1)}, s32[1536]{0:T(1024)}, u32[]{:S(2)}) copy-start(s32[1536]{0:T(1024)} %get-tuple-element.6) | copy-start | bytes 18436
  247.3 32.1 %copy-start.20 = (pred[1536]{0:T(1024)(128)(4,1)S(1)}, pred[1536]{0:T(1024)(128)(4,1)}, u32[]{:S(2)}) copy-start(pred[1536]{0:T(1024)(128)(4,1)} %fusion.125) | copy-start | bytes 4612
where the time goes:
time: 421 us; the launch traced here: 416 us
  other arithmetic  172 us (41%)
  matrix products  146 us (35%)
  local copies, waits for them, and re-layouts  66.3 us (16%)
  starting transfers between devices  12.9 us (3%)
  blocking collectives  10.6 us (3%)
  waiting for transfers between devices  6.83 us (2%)
    dot_general x1, matrix products, shards(): lax.dot_general(weighted, basis_rows, (((0,), (0,)), ((), ())), preferred...  136 us
    dot_general x1, other arithmetic, shards(): lax.dot_general(basis_rows, flat_grid, (((1,), (1,)), ((), ())), preferre...  135 us
    gather x3, local copies, waits for them, and re-layouts, shards(): jnp.take(helm_table, degree, axis=1)  22.7 us
    mul x7, other arithmetic, shards(): summed = summed + coefficient[None] * window  18.8 us
    convert_element_type x1, other arithmetic, shards(): arrival = summed.astype(jnp.bfloat16)  10.6 us
    all_to_all x1, blocking collectives, shards(): lax.all_to_all(outgoing, ('lat', 'lev'), split_axis=0, concat_axis=0, til...  10.6 us
    gather x1, local copies, waits for them, and re-layouts, shards(): first_wave = jnp.take(pair_order, slot_ident, axis=0)  9.48 us
  transfers between devices with their start and end apart: 3, of which 1 were waited for; matrix products, arithmetic and copies ran while one was open for 47% of the time, Pallas kernels for 0%

commit v1 on v0

v1 whole, which is shorter than its diff:
```python
import functools
import math

import jax
import jax.numpy as jnp
import numpy as np
from jax import lax
from jax.experimental import pallas as pl
from jax.experimental.pallas import tpu as pltpu
from jax.sharding import PartitionSpec as P

HMAX = 12
LANES = 128
GROUP = 8


@functools.lru_cache(maxsize=None)
def tables(lon_count, wave_count):
    quarter = lon_count // 4
    classes = [np.arange(k, wave_count, 4) for k in (0, 2)]
    odd = np.arange(1, wave_count, 2)
    column = np.arange(quarter)
    norm = 1.0 / math.sqrt(lon_count)
    built = []
    for waves in classes:
        angle = (waves[:, None] * column[None, :] % lon_count) * (2.0 * math.pi / lon_count)
        built.append(np.stack([np.cos(angle), -np.sin(angle)]) * norm)
    angle = (odd[:, None] * column[None, :] % lon_count) * (2.0 * math.pi / lon_count)
    sign = np.where(odd % 4 == 1, 1.0, -1.0)[:, None]
    cos, sin = np.cos(angle), np.sin(angle)
    real = np.concatenate([cos, -sign * sin], axis=1)
    imag = np.concatenate([-sin, -sign * cos], axis=1)
    built.append(np.stack([real, imag]) * norm)
    order = np.concatenate(classes + [odd]).astype(np.int32)
    return [t.astype(np.float32).astype(jnp.bfloat16) for t in built], order


def interp_kernel(low_ref, mid_ref, high_ref, offset_ref, weight_ref, out_ref, wide):
    fields, rows, width = mid_ref.shape
    for f in range(fields):
        for i, ref in enumerate((low_ref, mid_ref, high_ref)):
            wide[f, i * rows : (i + 1) * rows, :] = ref[f].astype(jnp.float32)

    def chunk(step, carry):
        here = pl.ds(pl.multiple_of(step * LANES, LANES), LANES)
        offset = offset_ref[:, here]
        weights = [weight_ref[k, :, here].astype(jnp.float32) for k in range(4)]
        totals = [jnp.zeros((rows, LANES), jnp.float32) for _ in range(fields)]
        picks = [offset == start for start in range(-HMAX, HMAX - 2)]
        for shift in range(-HMAX, HMAX + 1):
            coefficient = jnp.zeros((rows, LANES), jnp.float32)
            for k in range(4):
                start = shift - k
                if -HMAX <= start < HMAX - 2:
                    coefficient = jnp.where(picks[start + HMAX], weights[k], coefficient)
            for f in range(fields):
                totals[f] = totals[f] + coefficient * wide[f, pl.ds(rows + shift, rows), here]
        for f in range(fields):
            out_ref[f, :, here] = totals[f].astype(out_ref.dtype)
        return carry

    lax.fori_loop(0, width // LANES, chunk, 0)


def interpolate(low, mid, high, offset, weights):
    fields, rows, lon_count = mid.shape
    width = lon_count // 4

    def block(lead):
        return pl.BlockSpec((lead, rows, width), lambda i: (0, 0, i))

    return pl.pallas_call(
        interp_kernel,
        grid=(lon_count // width,),
        out_shape=jax.ShapeDtypeStruct(mid.shape, mid.dtype),
        in_specs=[
            block(fields),
            block(fields),
            block(fields),
            pl.BlockSpec((rows, width), lambda i: (0, i)),
            block(4),
        ],
        out_specs=block(fields),
        scratch_shapes=[pltpu.VMEM((fields, 3 * rows, width), jnp.float32)],
        compiler_params=pltpu.CompilerParams(vmem_limit_bytes=32 * 1024 * 1024),
    )(low, mid, high, offset, weights)


def spectral_kernel(wave_count, level_count, pair_ref, table_ref, shifted_ref, leg_ref, in_ref, out_ref):
    pair = pair_ref[pl.program_id(0)]
    slots = leg_ref.shape[1]
    half = level_count * GROUP
    legendre = leg_ref[0]
    projected = lax.dot_general(
        in_ref[0], legendre, (((1,), (1,)), ((), ())), preferred_element_type=jnp.float32
    )
    table = table_ref[...]
    rolled = pltpu.roll(table, table.shape[1] - pair, 1)[:, :slots]
    upper = shifted_ref[:, :slots]

    def lower_mask(rows):
        return lax.broadcasted_iota(jnp.int32, (rows, slots), 1) < wave_count - pair

    operator = jnp.where(lower_mask(level_count * level_count), rolled, upper)
    mask = lower_mask(half)
    chosen = jnp.where(mask, projected[:half], projected[half:])
    solved = []
    for v in range(level_count):
        total = jnp.zeros((GROUP, slots), jnp.float32)
        for w in range(level_count):
            row = v * level_count + w
            total = total + operator[row : row + 1] * chosen[w * GROUP : (w + 1) * GROUP]
        solved.append(total)
    solved = jnp.concatenate(solved, axis=0)
    placed = jnp.concatenate([jnp.where(mask, solved, 0.0), jnp.where(mask, 0.0, solved)], axis=0)
    returned = jnp.dot(
        placed.astype(jnp.bfloat16), legendre, preferred_element_type=jnp.float32
    )
    out_ref[0] = returned.astype(out_ref.dtype)


def spectral(pair_here, helmholtz, legendre, stacked):
    pair_local, slot_count, lat_total = legendre.shape
    wave_count, level_count, _ = helmholtz.shape
    rows = stacked.shape[1]
    span = -(-slot_count // 256) * 256
    flat = helmholtz.reshape(wave_count, level_count * level_count).T
    table = jnp.pad(flat, ((0, 0), (0, span - wave_count)))
    shifted = jnp.pad(flat, ((0, 0), (1, span - wave_count - 1)))
    whole = pl.BlockSpec(table.shape, lambda i, pair: (0, 0))
    return pl.pallas_call(
        functools.partial(spectral_kernel, wave_count, level_count),
        grid_spec=pltpu.PrefetchScalarGridSpec(
            num_scalar_prefetch=1,
            grid=(pair_local,),
            in_specs=[
                whole,
                whole,
                pl.BlockSpec((1, slot_count, lat_total), lambda i, pair: (i, 0, 0)),
                pl.BlockSpec((1, rows, lat_total), lambda i, pair: (i, 0, 0)),
            ],
            out_specs=pl.BlockSpec((1, rows, lat_total), lambda i, pair: (i, 0, 0)),
        ),
        out_shape=jax.ShapeDtypeStruct(stacked.shape, stacked.dtype),
        compiler_params=pltpu.CompilerParams(vmem_limit_bytes=32 * 1024 * 1024),
    )(pair_here, table, shifted, legendre, stacked)


def shards(grid_old, depart_offset, interp_weights, pair_order, legendre, helmholtz):
    lat_count = lax.axis_size("lat")
    lev_count = lax.axis_size("lev")
    fields, lev_local, row_count, lon_count = grid_old.shape
    pair_count = pair_order.shape[0]
    pair_local, slot_count, lat_total = legendre.shape
    wave_count = helmholtz.shape[0]
    level_count = helmholtz.shape[1]
    local = fields * lev_local * row_count
    quarter = lon_count // 4
    assert row_count >= HMAX and 2 * fields <= GROUP
    (basis0, basis2, basis_odd), order = tables(lon_count, wave_count)
    count0, count2 = basis0.shape[1], basis2.shape[1]

    forward = [(i, i + 1) for i in range(lat_count - 1)]
    backward = [(i + 1, i) for i in range(lat_count - 1)]
    low = lax.ppermute(grid_old, "lat", forward)
    high = lax.ppermute(grid_old, "lat", backward)
    arrival = jnp.stack(
        [
            interpolate(
                low[:, v], grid_old[:, v], high[:, v], depart_offset[v], interp_weights[:, v]
            )
            for v in range(lev_local)
        ],
        axis=1,
    )
    flat = arrival.reshape(local, lon_count).astype(jnp.float32)
    f0, f1, f2, f3 = [flat[:, a * quarter : (a + 1) * quarter] for a in range(4)]
    even, swing = f0 + f2, f1 + f3
    kind = jnp.bfloat16
    sum0 = (even + swing).astype(kind)
    sum2 = (even - swing).astype(kind)
    odd = jnp.concatenate([(f0 - f2).astype(kind), (f1 - f3).astype(kind)], axis=1)

    def project(basis, part):
        return lax.dot_general(
            basis, part, (((2,), (1,)), ((), ())), preferred_element_type=jnp.float32
        ).astype(kind)

    fourier = jnp.concatenate(
        [project(basis0, sum0), project(basis2, sum2), project(basis_odd, odd)], axis=1
    )
    waves = jnp.stack([pair_order, wave_count - 1 - pair_order], axis=1).reshape(-1)
    match = waves[:, None] == order[None, :]
    select = match.astype(kind)
    sent = jnp.concatenate(
        [
            jnp.dot(select, fourier[c], preferred_element_type=jnp.float32).astype(kind)
            for c in range(2)
        ],
        axis=1,
    )
    moved = lax.all_to_all(sent, ("lat", "lev"), split_axis=0, concat_axis=0, tiled=True)
    moved = moved.reshape(
        lat_count, lev_count, pair_local, 2, 2 * fields, lev_local, row_count
    )
    stacked = moved.transpose(2, 3, 1, 5, 4, 0, 6)
    stacked = stacked.reshape(pair_local, 2, level_count, 2 * fields, lat_total)
    stacked = jnp.pad(stacked, ((0, 0),) * 3 + ((0, GROUP - 2 * fields), (0, 0)))
    stacked = stacked.reshape(pair_local, 2 * level_count * GROUP, lat_total)
    holder = lax.axis_index("lat") * lev_count + lax.axis_index("lev")
    pair_here = lax.dynamic_slice_in_dim(pair_order, holder * pair_local, pair_local)
    returned = spectral(pair_here, helmholtz, legendre, stacked)
    returned = returned.reshape(pair_local, 2, level_count, GROUP, lat_total)[:, :, :, : 2 * fields]
    returned = returned.reshape(
        pair_local, 2, lev_count, lev_local, 2 * fields, lat_count, row_count
    )
    outgoing = returned.transpose(5, 2, 0, 1, 4, 3, 6).reshape(pair_count * 2, 2 * local)
    arrived = lax.all_to_all(outgoing, ("lat", "lev"), split_axis=0, concat_axis=0, tiled=True)
    gain = jnp.where(match, np.where(order == 0, 1.0, 2.0).astype(np.float32)[None, :], 0.0)
    natural = lax.dot_general(
        gain.astype(kind), arrived, (((0,), (0,)), ((), ())), preferred_element_type=jnp.float32
    ).astype(kind)

    def rebuild(basis, first):
        total = 0.0
        for c in range(2):
            rows = natural[first : first + basis.shape[1], c * local : (c + 1) * local]
            total = total + lax.dot_general(
                rows, basis[c], (((0,), (0,)), ((), ())), preferred_element_type=jnp.float32
            )
        return total

    back0 = rebuild(basis0, 0)
    back2 = rebuild(basis2, count0)
    back_odd = rebuild(basis_odd, count0 + count2)
    plus, minus = back0 + back2, back0 - back2
    left, right = back_odd[:, :quarter], back_odd[:, quarter:]
    rebuilt = jnp.concatenate([plus + left, minus + right, plus - left, minus - right], axis=1)
    return rebuilt.astype(kind).reshape(fields, lev_local, row_count, lon_count)


def solution(mesh):
    in_specs = (
        P(None, "lev", "lat", None),
        P("lev", "lat", None),
        P(None, "lev", "lat", None),
        P(),
        P(("lat", "lev"), None, None),
        P(),
    )
    out_specs = P(None, "lev", "lat", None)
    return jax.shard_map(shards, mesh=mesh, in_specs=in_specs, out_specs=out_specs, check_vma=False)
```

time: 421 us -> 87.7 us (0.21); the launches traced: 416 us -> 87.2 us
  other arithmetic: 172 us -> 1.78 us
  matrix products: 146 us -> 5.59 us
  local copies, waits for them, and re-layouts: 66.3 us -> 17.8 us
  waiting for transfers between devices: 6.83 us -> 26.1 us
  Pallas kernels: 0 us -> 11 us
    dot_general x4 -> x12, matrix products: 146 us -> 5.59 us  [the longest x3 2.07 us: project(): lax.dot_general(basis, part, (((2,), (1,)), ((), ())), preferred_element_...]
    dot_general x1 -> x0, other arithmetic: 135 us -> none  [shards(): lax.dot_general(basis_rows, flat_grid, (((1,), (1,)), ((), ())), preferre...]
    gather x5 -> x0, local copies, waits for them, and re-layouts: 32.8 us -> none  [the longest x3 22.7 us: shards(): jnp.take(helm_table, degree, axis=1)]
    mul x8 -> x0, other arithmetic: 19.1 us -> none  [the longest x7 18.8 us: shards(): summed = summed + coefficient[None] * window]
    ppermute x2, waiting for transfers between devices: 0.01 us -> 17.7 us  [the longest x1 17.7 us: shards(): low = lax.ppermute(grid_old, 'lat', forward)]
    reshape x8 -> x3, local copies, waits for them, and re-layouts: 14.8 us -> 2.7 us  [the longest x1 1.94 us: shards(): moved.reshape(lat_count, lev_count, pair_local, 2, 2 * fields, lev_local,...]
    convert_element_type x2, other arithmetic: 11.2 us -> 0.15 us  [the longest x1 0.1 us: shards(): flat = arrival.reshape(local, lon_count).astype(jnp.float32)]
    pallas_call x0 -> x2, Pallas kernels: none -> 11 us  [the longest x1 5.97 us: interpolate(): pl.pallas_call(interp_kernel, grid=(lon_count // width,), out_shape=jax.S...]
  transfers between devices with their start and end apart: 3 -> 3, of which waited for: 1 -> 2; matrix products, arithmetic and copies ran while one was open for 47% -> 3% of each run, Pallas kernels for 0% -> 0%
where the time goes in v1:
time: 87.7 us; the launch traced here: 87.2 us
  waiting for transfers between devices  26.1 us (30%)
  local copies, waits for them, and re-layouts  17.8 us (20%)
  starting transfers between devices  13.2 us (15%)
  blocking collectives  11.4 us (13%)
  Pallas kernels  11 us (13%)
  matrix products  5.59 us (6%)
  other arithmetic  1.78 us (2%)
    ppermute x1, waiting for transfers between devices, shards(): low = lax.ppermute(grid_old, 'lat', forward)  17.7 us
    all_to_all x1, blocking collectives, shards(): lax.all_to_all(outgoing, ('lat', 'lev'), split_axis=0, concat_axis=0, til...  11.4 us
    unnamed x35, local copies, waits for them, and re-layouts  11.1 us
    all_to_all x1, waiting for transfers between devices, shards(): lax.all_to_all(sent, ('lat', 'lev'), split_axis=0, concat_axis=0, tiled=T...  8.36 us
    all_to_all x1, starting transfers between devices, shards(): lax.all_to_all(sent, ('lat', 'lev'), split_axis=0, concat_axis=0, tiled=T...  7.93 us
    pallas_call x1, Pallas kernels, interpolate(): pl.pallas_call(interp_kernel, grid=(lon_count // width,), out_shape=jax.S...  5.97 us
    pallas_call x1, Pallas kernels, spectral(): pl.pallas_call(functools.partial(spectral_kernel, wave_count, level_count...  5.02 us
    ppermute x1, starting transfers between devices, shards(): low = lax.ppermute(grid_old, 'lat', forward)  3.99 us
  transfers between devices with their start and end apart: 3, of which 2 were waited for; matrix products, arithmetic and copies ran while one was open for 3% of the time, Pallas kernels for 0%

profile of v1, /device:TPU:1, one launch (start us, length us, event | category | flops | bytes accessed | tf_op | source)
XLA Modules:
  0.0 87.2 jit_solution(3293560572028649683)
XLA Ops:
  0.0 4.0 %collective-permute-start = (bf16[3,1,16,5120]{3,2,0,1:T(8,128)(2,1)}, bf16[3,1,16,5120]{3,2,0,1:T(8,128)(2,1)S(1)}, u32[]{:S(2)}, u32[]{:S(2)}) collective-permute-start(bf16[3,1,16,5120]{3,2,0,1:T(8,128)(2,1)} %bitcast.74), channel_id=1, source_target_pairs={{0,4},{4,8},{8,12},{12,16},{16,20},{20,24},{24,28},{1,5},{5,9},{9,... | collective-permute-start | bytes 1474568 | tf_op jit(solution)/shard_map/ppermute | solution.py:165
  4.0 1.3 %collective-permute-start.1 = (bf16[3,1,16,5120]{3,2,0,1:T(8,128)(2,1)}, bf16[3,1,16,5120]{3,2,0,1:T(8,128)(2,1)S(1)}, u32[]{:S(2)}, u32[]{:S(2)}) collective-permute-start(bf16[3,1,16,5120]{3,2,0,1:T(8,128)(2,1)} %bitcast.75), channel_id=1, source_target_pairs={{4,0},{8,4},{12,8},{16,12},{20,16},{24,20},{28,24},{5,1},{9,5},{13... | collective-permute-start | bytes 1474568 | tf_op jit(solution)/shard_map/ppermute | solution.py:166
  5.3 0.7 stack.9
  6.0 0.7 broadcast_subtract_fusion
  6.7 0.1 copy.25
  6.8 0.1 eq.17
  7.0 17.7 %collective-permute-done = bf16[3,1,16,5120]{3,2,0,1:T(8,128)(2,1)S(1)} collective-permute-done((bf16[3,1,16,5120]{3,2,0,1:T(8,128)(2,1)}, bf16[3,1,16,5120]{3,2,0,1:T(8,128)(2,1)S(1)}, u32[]{:S(2)}, u32[]{:S(2)}) %collective-permute-start) | collective-permute-done | bytes 491552 | tf_op jit(solution)/shard_map/ppermute | solution.py:165
  24.7 1.1 %copy-done.1 = bf16[4,1,16,5120]{3,2,1,0:T(8,128)(2,1)S(1)} copy-done((bf16[4,1,16,5120]{3,2,1,0:T(8,128)(2,1)S(1)}, bf16[4,1,16,5120]{3,2,1,0:T(8,128)(2,1)}, u32[]{:S(2)}) %copy-start.1) | copy-done | bytes 655384
  25.8 1.0 %copy-done.2 = bf16[3,1,16,5120]{3,2,1,0:T(8,128)(2,1)S(1)} copy-done((bf16[3,1,16,5120]{3,2,1,0:T(8,128)(2,1)S(1)}, bf16[3,1,16,5120]{3,2,1,0:T(8,128)(2,1)}, u32[]{:S(2)}) %copy-start.2) | copy-done | bytes 491544
  26.8 1.0 %copy-done.3 = s32[1,16,5120]{2,1,0:T(8,128)S(1)} copy-done((s32[1,16,5120]{2,1,0:T(8,128)S(1)}, s32[1,16,5120]{2,1,0:T(8,128)}, u32[]{:S(2)}) %copy-start.3) | copy-done | bytes 327704
  27.8 6.0 %shard_map.163 = bf16[3,16,5120]{2,1,0:T(8,128)(2,1)S(1)} custom-call(bf16[3,16,5120]{2,1,0:T(8,128)(2,1)S(1)} %bitcast.77, bf16[3,16,5120]{2,1,0:T(8,128)(2,1)S(1)} %bitcast.76, bf16[3,16,5120]{2,1,0:T(8,128)(2,1)S(1)} %bitcast.78, s32[16,5120]{1,0:T(8,128)S(1)} %bitcast.79, bf16[4,16,5120]{2,1,0:T(8,128)(2,1)S(1)} %bitcast.73), custom_call_target="tpu_custom_call" | custom-call | tf_op jit(solution)/shard_map/pallas_call | solution.py:72
  33.8 0.0 copy-start.4
  33.8 0.1 bitcast_convert_fusion
  33.9 0.1 subtract_convert_fusion.3
  34.0 0.4 fusion.25
  34.4 0.4 fusion.26
  34.8 1.1 %copy-done.4 = bf16[2,384,2560]{2,1,0:T(8,128)(2,1)S(1)} copy-done((bf16[2,384,2560]{2,1,0:T(8,128)(2,1)S(1)}, bf16[2,384,2560]{2,1,0:T(8,128)(2,1)}, u32[]{:S(2)}) %copy-start.4) | copy-done | bytes 3932184
  35.9 1.2 %fusion.24 = bf16[2,384,48]{1,2,0:T(8,128)(2,1)S(1)} fusion(bf16[2,384,2560]{2,1,0:T(8,128)(2,1)S(1)} %copy-done.4, bf16[48,1280]{1,0:T(8,128)(2,1)S(1)} %get-tuple-element.10, bf16[48,1280]{1,0:T(8,128)(2,1)S(1)} %get-tuple-element.9), kind=kOutput, calls=%fused_computation.22 | convolution fusion | flops 189272064 | bytes 4251648 | tf_op jit(solution)/shard_map/dot_general | solution.py:185
  37.1 0.1 pad_maximum_fusion.1
  37.2 0.6 fusion.18
  37.8 0.6 fusion.21
  38.5 0.8 copy.28
  39.3 7.9 %all-to-all-start = ((bf16[32,24,96]{2,1,0:T(8,128)(2,1)}), bf16[32,24,96]{2,1,0:T(8,128)(2,1)S(1)}, u32[]{:S(2)}, u32[]{:S(2)}) async-start(bf16[32,24,96]{2,1,0:T(8,128)(2,1)} %bitcast.18), calls=%async_computation | async-start | bytes 393216 | tf_op jit(solution)/shard_map/all_to_all | solution.py:202
  47.3 0.8 dynamic_slice.3.pair_ref
  48.0 0.1 fusion.44
  48.1 8.4 %all-to-all-done = bf16[32,24,96]{2,1,0:T(8,128)(2,1)S(1)} async-done(((bf16[32,24,96]{2,1,0:T(8,128)(2,1)}), bf16[32,24,96]{2,1,0:T(8,128)(2,1)S(1)}, u32[]{:S(2)}, u32[]{:S(2)}) %all-to-all-start) | async-done | bytes 147488 | tf_op jit(solution)/shard_map/all_to_all | solution.py:202
  56.5 1.9 %reshape.89 = bf16[8,4,12,2,6,1,16]{6,4,3,2,1,0,5:T(8,128)(2,1)} reshape(bf16[32,24,96]{2,1,0:T(8,128)(2,1)S(1)} %all-to-all-done) | data formatting | bytes 294912 | tf_op jit(solution)/shard_map/reshape | solution.py:203
  58.4 4.0 %copy.39 = bf16[12,2,4,1,6,8,16]{6,5,4,2,1,0,3:T(8,128)(2,1)} copy(bf16[12,2,4,1,6,8,16]{6,4,1,0,2,5,3:T(8,128)(2,1)} %bitcast.80) | data formatting | bytes 294912
  62.4 2.1 %reshape.98 = bf16[12,2,4,6,128]{4,3,2,1,0:T(8,128)(2,1)S(1)} reshape(bf16[12,2,4,1,6,8,16]{6,5,4,2,1,0,3:T(8,128)(2,1)} %copy.39) | data formatting | bytes 294912
  64.6 5.0 %shard_map.164 = bf16[12,64,128]{2,1,0:T(8,128)(2,1)S(1)} custom-call(s32[12]{0:T(128)S(1)} %dynamic_slice.3.pair_ref, f32[16,1024]{1,0:T(8,128)S(1)} %get-tuple-element.12.table_ref, f32[16,1024]{1,0:T(8,128)S(1)} %get-tuple-element.11.shifted_ref, bf16[12,769,128]{2,1,0:T(8,128)(2,1)S(1)} %copy-done, bf16[12,64,128]{2,1,0:T(8,128)(2,1)S(1)} %bitcast.71), custom_call_target="tpu_custom_call" | custom-call | tf_op jit(solution)/shard_map/pallas_call | solution.py:131
  69.6 0.1 copy.37
  69.7 0.7 reshape.93
  70.4 0.0 copy-start.15
  70.4 0.5 copy.32
  71.0 0.8 all_to_all.16
  71.8 11.4 %all_to_all.21 = bf16[32,24,96]{2,1,0:T(8,128)(2,1)S(1)} all-to-all(bf16[32,24,96]{2,1,0:T(8,128)(2,1)S(1)} %all_to_all.16), channel_id=1, replica_groups=mesh['lat'=8,'lev'=4] {'lat','lev'}, dimensions={0} | all-to-all | bytes 294912 | tf_op jit(solution)/shard_map/all_to_all | solution.py:218
  83.2 0.5 fusion.15
  83.7 0.2 fusion.37
  84.0 0.0 copy-start.6
  84.0 0.4 fusion.34
  84.4 0.3 copy-done.10
  84.7 0.2 fusion.40
  84.9 0.3 convolution_add_fusion.1
  85.2 0.4 copy-done.6
  85.6 0.5 convolution_add_fusion
  86.1 0.1 copy-done.12
  86.1 0.2 add_convert_fusion.1
  86.4 0.8 pad_maximum_fusion
  (28 shorter events, 0.2 us)
Async XLA Ops:
  0.0 24.7 %collective-permute-start = (bf16[3,1,16,5120]{3,2,0,1:T(8,128)(2,1)}, bf16[3,1,16,5120]{3,2,0,1:T(8,128)(2,1)S(1)}, u32[]{:S(2)}, u32[]{:S(2)}) collective-permute-start(bf16[3,1,16,5120]{3,2,0,1:T(8,128)(2,1)} %bitcast.74), channel_id=1, source_target_pairs={{0,4},{4,8},{8,12},{12,16},{16,20},{20,24},{24,28},{1,5},{5,9},{9,... | collective-permute-start | bytes 1474568 | tf_op jit(solution)/shard_map/ppermute | solution.py:165
  4.0 20.7 %collective-permute-start.1 = (bf16[3,1,16,5120]{3,2,0,1:T(8,128)(2,1)}, bf16[3,1,16,5120]{3,2,0,1:T(8,128)(2,1)S(1)}, u32[]{:S(2)}, u32[]{:S(2)}) collective-permute-start(bf16[3,1,16,5120]{3,2,0,1:T(8,128)(2,1)} %bitcast.75), channel_id=1, source_target_pairs={{4,0},{8,4},{12,8},{16,12},{20,16},{24,20},{28,24},{5,1},{9,5},{13... | collective-permute-start | bytes 1474568 | tf_op jit(solution)/shard_map/ppermute | solution.py:166
  24.7 1.1 %copy-start.1 = (bf16[4,1,16,5120]{3,2,1,0:T(8,128)(2,1)S(1)}, bf16[4,1,16,5120]{3,2,1,0:T(8,128)(2,1)}, u32[]{:S(2)}) copy-start(bf16[4,1,16,5120]{3,2,1,0:T(8,128)(2,1)} %param.19) | copy-start | bytes 1966084
  25.8 1.0 %copy-start.2 = (bf16[3,1,16,5120]{3,2,1,0:T(8,128)(2,1)S(1)}, bf16[3,1,16,5120]{3,2,1,0:T(8,128)(2,1)}, u32[]{:S(2)}) copy-start(bf16[3,1,16,5120]{3,2,1,0:T(8,128)(2,1)} %param.17) | copy-start | bytes 1474564
  26.8 1.0 %copy-start.3 = (s32[1,16,5120]{2,1,0:T(8,128)S(1)}, s32[1,16,5120]{2,1,0:T(8,128)}, u32[]{:S(2)}) copy-start(s32[1,16,5120]{2,1,0:T(8,128)} %param.18) | copy-start | bytes 983044
  27.8 6.2 %copy-start.7 = (bf16[2,192,1280]{2,1,0:T(8,128)(2,1)S(1)}, bf16[2,192,1280]{2,1,0:T(8,128)(2,1)}, u32[]{:S(2)}) copy-start(bf16[2,192,1280]{2,1,0:T(8,128)(2,1)} %constant.46.clone) | copy-start | bytes 2949124
  27.8 6.6 %copy-start.8 = (bf16[2,192,1280]{2,1,0:T(8,128)(2,1)S(1)}, bf16[2,192,1280]{2,1,0:T(8,128)(2,1)}, u32[]{:S(2)}) copy-start(bf16[2,192,1280]{2,1,0:T(8,128)(2,1)} %constant.47.clone) | copy-start | bytes 2949124
  33.8 2.1 %copy-start.4 = (bf16[2,384,2560]{2,1,0:T(8,128)(2,1)S(1)}, bf16[2,384,2560]{2,1,0:T(8,128)(2,1)}, u32[]{:S(2)}) copy-start(bf16[2,384,2560]{2,1,0:T(8,128)(2,1)} %constant.48.clone) | copy-start | bytes 11796484
  35.9 1.4 %copy-start.14 = (s32[768]{0:T(1024)S(1)}, s32[768]{0:T(1024)}, u32[]{:S(2)}) copy-start(s32[768]{0:T(1024)} %constant.67) | copy-start | bytes 9220
  37.1 10.9 %copy-start.13 = (f32[768,4,4]{0,2,1:T(4,128)S(1)}, f32[768,4,4]{0,2,1:T(4,128)}, u32[]{:S(2)}) copy-start(f32[768,4,4]{0,2,1:T(4,128)} %param.22) | copy-start | bytes 147460
  39.3 17.2 %all-to-all-start = ((bf16[32,24,96]{2,1,0:T(8,128)(2,1)}), bf16[32,24,96]{2,1,0:T(8,128)(2,1)S(1)}, u32[]{:S(2)}, u32[]{:S(2)}) async-start(bf16[32,24,96]{2,1,0:T(8,128)(2,1)} %bitcast.18), calls=%async_computation | async-start | bytes 393216 | tf_op jit(solution)/shard_map/all_to_all | solution.py:202
  58.4 6.2 %copy-start = (bf16[12,769,128]{2,1,0:T(8,128)(2,1)S(1)}, bf16[12,769,128]{2,1,0:T(8,128)(2,1)}, u32[]{:S(2)}) copy-start(bf16[12,769,128]{2,1,0:T(8,128)(2,1)} %leg_ref.1) | copy-start | bytes 7087108
  70.4 12.8 %copy-start.15 = (bf16[768]{0:T(1024)(128)(2,1)S(1)}, bf16[768]{0:T(1024)(128)(2,1)}, u32[]{:S(2)}) copy-start(bf16[768]{0:T(1024)(128)(2,1)} %constant.106) | copy-start | bytes 4612
  71.0 12.7 %copy-start.11 = (bf16[192,1280]{1,0:T(8,128)(2,1)S(1)}, bf16[192,1280]{1,0:T(8,128)(2,1)}, u32[]{:S(2)}) copy-start(bf16[192,1280]{1,0:T(8,128)(2,1)} %constant.53.clone) | copy-start | bytes 1474564
  71.8 12.2 %copy-start.5 = (bf16[384,2560]{1,0:T(8,128)(2,1)S(1)}, bf16[384,2560]{1,0:T(8,128)(2,1)}, u32[]{:S(2)}) copy-start(bf16[384,2560]{1,0:T(8,128)(2,1)} %constant.55.clone) | copy-start | bytes 5898244
  83.7 1.0 %copy-start.10 = (bf16[192,1280]{1,0:T(8,128)(2,1)S(1)}, bf16[192,1280]{1,0:T(8,128)(2,1)}, u32[]{:S(2)}) copy-start(bf16[192,1280]{1,0:T(8,128)(2,1)} %constant.51.clone) | copy-start | bytes 1474564
  83.7 1.2 %copy-start.9 = (bf16[192,1280]{1,0:T(8,128)(2,1)S(1)}, bf16[192,1280]{1,0:T(8,128)(2,1)}, u32[]{:S(2)}) copy-start(bf16[192,1280]{1,0:T(8,128)(2,1)} %constant.54.clone) | copy-start | bytes 1474564
  84.0 1.6 %copy-start.6 = (bf16[384,2560]{1,0:T(8,128)(2,1)S(1)}, bf16[384,2560]{1,0:T(8,128)(2,1)}, u32[]{:S(2)}) copy-start(bf16[384,2560]{1,0:T(8,128)(2,1)} %constant.56.clone) | copy-start | bytes 5898244
  84.9 1.2 %copy-start.12 = (bf16[192,1280]{1,0:T(8,128)(2,1)S(1)}, bf16[192,1280]{1,0:T(8,128)(2,1)}, u32[]{:S(2)}) copy-start(bf16[192,1280]{1,0:T(8,128)(2,1)} %constant.52.clone) | copy-start | bytes 1474564

commit v2 on v1

--- a/solution.py
+++ b/solution.py
@@ -12,6 +12,7 @@
 HMAX = 12
 LANES = 128
 GROUP = 8
+EDGE = 4
 
 
 @functools.lru_cache(maxsize=None)
@@ -38,8 +39,12 @@
 def interp_kernel(low_ref, mid_ref, high_ref, offset_ref, weight_ref, out_ref, wide):
     fields, rows, width = mid_ref.shape
     for f in range(fields):
-        for i, ref in enumerate((low_ref, mid_ref, high_ref)):
-            wide[f, i * rows : (i + 1) * rows, :] = ref[f].astype(jnp.float32)
+        wide[f, rows : 2 * rows, :] = mid_ref[f].astype(jnp.float32)
+        for first, ref in ((rows - HMAX, low_ref), (2 * rows, high_ref)):
+            for g in range(HMAX // EDGE):
+                start = first + g * EDGE
+                part = ref[f * (HMAX // EDGE) + g]
+                wide[f, start : start + EDGE, :] = part.astype(jnp.float32)
 
     def chunk(step, carry):
         here = pl.ds(pl.multiple_of(step * LANES, LANES), LANES)
@@ -69,14 +74,15 @@
     def block(lead):
         return pl.BlockSpec((lead, rows, width), lambda i: (0, 0, i))
 
+    edge = pl.BlockSpec((low.shape[0], EDGE, width), lambda i: (0, 0, i))
     return pl.pallas_call(
         interp_kernel,
         grid=(lon_count // width,),
         out_shape=jax.ShapeDtypeStruct(mid.shape, mid.dtype),
         in_specs=[
+            edge,
             block(fields),
-            block(fields),
-            block(fields),
+            edge,
             pl.BlockSpec((rows, width), lambda i: (0, i)),
             block(4),
         ],
@@ -86,13 +92,46 @@
     )(low, mid, high, offset, weights)
 
 
-def spectral_kernel(wave_count, level_count, pair_ref, table_ref, shifted_ref, leg_ref, in_ref, out_ref):
+def spectral_kernel(wave_count, level_count, pair_ref, table_ref, shifted_ref, leg_ref, in_ref, out_ref, lines):
     pair = pair_ref[pl.program_id(0)]
     slots = leg_ref.shape[1]
     half = level_count * GROUP
     legendre = leg_ref[0]
+    local_rows = in_ref.shape[1]
+
+    @pl.when(pl.program_id(0) == 0)
+    def _():
+        tile = lax.broadcasted_iota(jnp.int32, (local_rows, LANES), 1) // (LANES // GROUP)
+        for g in range(lines.shape[0]):
+            for level in range(level_count):
+                parts = [
+                    in_ref[(g * GROUP + i) * level_count + level].astype(jnp.float32)
+                    for i in range(GROUP)
+                ]
+                for bit in (1, 2, 4):
+                    low_side = (tile & bit) == 0
+                    step = bit * (LANES // GROUP)
+                    for i in range(GROUP):
+                        if i & bit == 0:
+                            a, b = parts[i], parts[i + bit]
+                            parts[i] = jnp.where(low_side, a, pltpu.roll(b, step, 1))
+                            parts[i + bit] = jnp.where(
+                                low_side, pltpu.roll(a, LANES - step, 1), b
+                            )
+                for i in range(GROUP):
+                    first = (level * GROUP + i) * local_rows
+                    lines[g, first : first + local_rows, :] = parts[i]
+
+    def gathered(which):
+        start = 2 * pl.program_id(0) + which
+        return jnp.concatenate(
+            [lines[g, pl.ds(start, half, stride=local_rows), :] for g in range(lines.shape[0])],
+            axis=1,
+        )
+
+    stacked = jnp.concatenate([gathered(0), gathered(1)], axis=0).astype(jnp.bfloat16)
     projected = lax.dot_general(
-        in_ref[0], legendre, (((1,), (1,)), ((), ())), preferred_element_type=jnp.float32
+        stacked, legendre, (((1,), (1,)), ((), ())), preferred_element_type=jnp.float32
     )
     table = table_ref[...]
     rolled = pltpu.roll(table, table.shape[1] - pair, 1)[:, :slots]
@@ -119,10 +158,10 @@
     out_ref[0] = returned.astype(out_ref.dtype)
 
 
-def spectral(pair_here, helmholtz, legendre, stacked):
+def spectral(pair_here, helmholtz, legendre, moved):
     pair_local, slot_count, lat_total = legendre.shape
     wave_count, level_count, _ = helmholtz.shape
-    rows = stacked.shape[1]
+    rows = 2 * level_count * GROUP
     span = -(-slot_count // 256) * 256
     flat = helmholtz.reshape(wave_count, level_count * level_count).T
     table = jnp.pad(flat, ((0, 0), (0, span - wave_count)))
@@ -137,13 +176,18 @@
                 whole,
                 whole,
                 pl.BlockSpec((1, slot_count, lat_total), lambda i, pair: (i, 0, 0)),
-                pl.BlockSpec((1, rows, lat_total), lambda i, pair: (i, 0, 0)),
+                pl.BlockSpec(moved.shape, lambda i, pair: (0, 0, 0)),
             ],
             out_specs=pl.BlockSpec((1, rows, lat_total), lambda i, pair: (i, 0, 0)),
+            scratch_shapes=[
+                pltpu.VMEM(
+                    (lat_total // LANES, level_count * GROUP * moved.shape[1], LANES), jnp.float32
+                )
+            ],
         ),
-        out_shape=jax.ShapeDtypeStruct(stacked.shape, stacked.dtype),
+        out_shape=jax.ShapeDtypeStruct((pair_local, rows, lat_total), moved.dtype),
         compiler_params=pltpu.CompilerParams(vmem_limit_bytes=32 * 1024 * 1024),
-    )(pair_here, table, shifted, legendre, stacked)
+    )(pair_here, table, shifted, legendre, moved)
 
 
 def shards(grid_old, depart_offset, interp_weights, pair_order, legendre, helmholtz):
@@ -156,23 +200,17 @@
     level_count = helmholtz.shape[1]
     local = fields * lev_local * row_count
     quarter = lon_count // 4
-    assert row_count >= HMAX and 2 * fields <= GROUP
+    assert row_count >= HMAX and 2 * fields <= GROUP and lev_local == 1
+    assert row_count * GROUP == LANES and lat_count % GROUP == 0
     (basis0, basis2, basis_odd), order = tables(lon_count, wave_count)
     count0, count2 = basis0.shape[1], basis2.shape[1]
 
     forward = [(i, i + 1) for i in range(lat_count - 1)]
     backward = [(i + 1, i) for i in range(lat_count - 1)]
-    low = lax.ppermute(grid_old, "lat", forward)
-    high = lax.ppermute(grid_old, "lat", backward)
-    arrival = jnp.stack(
-        [
-            interpolate(
-                low[:, v], grid_old[:, v], high[:, v], depart_offset[v], interp_weights[:, v]
-            )
-            for v in range(lev_local)
-        ],
-        axis=1,
-    )
+    groups = (fields * (HMAX // EDGE), EDGE, lon_count)
+    low = lax.ppermute(grid_old[:, 0, row_count - HMAX :].reshape(groups), "lat", forward)
+    high = lax.ppermute(grid_old[:, 0, :HMAX].reshape(groups), "lat", backward)
+    arrival = interpolate(low, grid_old[:, 0], high, depart_offset[0], interp_weights[:, 0])
     flat = arrival.reshape(local, lon_count).astype(jnp.float32)
     f0, f1, f2, f3 = [flat[:, a * quarter : (a + 1) * quarter] for a in range(4)]
     even, swing = f0 + f2, f1 + f3
@@ -196,20 +234,15 @@
         [
             jnp.dot(select, fourier[c], preferred_element_type=jnp.float32).astype(kind)
             for c in range(2)
-        ],
+        ]
+        + [jnp.zeros((2 * pair_count, LANES - 2 * local), kind)],
         axis=1,
     )
     moved = lax.all_to_all(sent, ("lat", "lev"), split_axis=0, concat_axis=0, tiled=True)
-    moved = moved.reshape(
-        lat_count, lev_count, pair_local, 2, 2 * fields, lev_local, row_count
-    )
-    stacked = moved.transpose(2, 3, 1, 5, 4, 0, 6)
-    stacked = stacked.reshape(pair_local, 2, level_count, 2 * fields, lat_total)
-    stacked = jnp.pad(stacked, ((0, 0),) * 3 + ((0, GROUP - 2 * fields), (0, 0)))
-    stacked = stacked.reshape(pair_local, 2 * level_count * GROUP, lat_total)
+    moved = moved.reshape(lat_count * lev_count, 2 * pair_local, LANES)
     holder = lax.axis_index("lat") * lev_count + lax.axis_index("lev")
     pair_here = lax.dynamic_slice_in_dim(pair_order, holder * pair_local, pair_local)
-    returned = spectral(pair_here, helmholtz, legendre, stacked)
+    returned = spectral(pair_here, helmholtz, legendre, moved)
     returned = returned.reshape(pair_local, 2, level_count, GROUP, lat_total)[:, :, :, : 2 * fields]
     returned = returned.reshape(
         pair_local, 2, lev_count, lev_local, 2 * fields, lat_count, row_count

time: 87.7 us -> 73.6 us (0.84)
  local copies, waits for them, and re-layouts: 17.8 us -> 7.39 us
  waiting for transfers between devices: 26.1 us -> 22.2 us
    unnamed x35, local copies, waits for them, and re-layouts: 11.1 us -> 2.2 us
    ppermute x2, waiting for transfers between devices: 17.7 us -> 13.2 us  [the longest x1 13.2 us: shards(): lax.ppermute(grid_old[:, 0, row_count - HMAX:].reshape(groups), 'lat', fo...]
    reshape x1 -> x0, local copies, waits for them, and re-layouts: 1.94 us -> none  [shards(): moved.reshape(lat_count, lev_count, pair_local, 2, 2 * fields, lev_local,...]
    slice x0 -> x1, local copies, waits for them, and re-layouts: none -> 1.4 us  [shards(): high = lax.ppermute(grid_old[:, 0, :HMAX].reshape(groups), 'lat', backward)]
  transfers between devices with their start and end apart: 3 -> 3, of which waited for: 2 -> 2; matrix products, arithmetic and copies ran while one was open for 3% -> 1% of each run, Pallas kernels for 0% -> 0%
where the time goes in v2:
time: 73.6 us; the launch traced here: 73.3 us
  waiting for transfers between devices  22.2 us (30%)
  starting transfers between devices  13.3 us (18%)
  Pallas kernels  11.8 us (16%)
  blocking collectives  11.4 us (15%)
  local copies, waits for them, and re-layouts  7.39 us (10%)
  matrix products  5.59 us (8%)
  other arithmetic  1.18 us (2%)
    ppermute x1, waiting for transfers between devices, shards(): lax.ppermute(grid_old[:, 0, row_count - HMAX:].reshape(groups), 'lat', fo...  13.2 us
    all_to_all x1, blocking collectives, shards(): lax.all_to_all(outgoing, ('lat', 'lev'), split_axis=0, concat_axis=0, til...  11.4 us
    all_to_all x1, waiting for transfers between devices, shards(): lax.all_to_all(sent, ('lat', 'lev'), split_axis=0, concat_axis=0, tiled=T...  9.04 us
    all_to_all x1, starting transfers between devices, shards(): lax.all_to_all(sent, ('lat', 'lev'), split_axis=0, concat_axis=0, tiled=T...  8.04 us
    pallas_call x1, Pallas kernels, interpolate(): pl.pallas_call(interp_kernel, grid=(lon_count // width,), out_shape=jax.S...  6.03 us
    pallas_call x1, Pallas kernels, spectral(): pl.pallas_call(functools.partial(spectral_kernel, wave_count, level_count...  5.76 us
    ppermute x1, starting transfers between devices, shards(): lax.ppermute(grid_old[:, 0, row_count - HMAX:].reshape(groups), 'lat', fo...  4 us
    unnamed x35, local copies, waits for them, and re-layouts  2.2 us
  transfers between devices with their start and end apart: 3, of which 2 were waited for; matrix products, arithmetic and copies ran while one was open for 1% of the time, Pallas kernels for 0%

profile of v2, /device:TPU:1, one launch (start us, length us, event | category | flops | bytes accessed | tf_op | source)
XLA Modules:
  0.0 73.3 jit_solution(9481972881054668081)
XLA Ops:
  0.0 1.4 %fusion.44 = (bf16[3,1,12,5120]{3,2,1,0:T(8,128)(2,1)S(1)}, bf16[3,1,12,5120]{3,2,1,0:T(8,128)(2,1)S(1)}) fusion(bf16[3,1,16,5120]{3,2,1,0:T(8,128)(2,1)} %param.17), kind=kLoop, calls=%fused_computation.61 | loop fusion | bytes 1474560 | tf_op jit(solution)/shard_map/slice | solution.py:212
  1.4 0.2 reshape_squeeze.6
  1.6 4.0 %collective-permute-start = (bf16[9,4,5120]{2,1,0:T(4,128)(2,1)S(1)}, bf16[9,4,5120]{2,1,0:T(4,128)(2,1)S(1)}, u32[]{:S(2)}, u32[]{:S(2)}) collective-permute-start(bf16[9,4,5120]{2,1,0:T(4,128)(2,1)S(1)} %reshape_squeeze.6), channel_id=1, source_target_pairs={{0,4},{4,8},{8,12},{12,16},{16,20},{20,24},{24,28},{1,5},{5,9},{9,... | collective-permute-start | bytes 1105928 | tf_op jit(solution)/shard_map/ppermute | solution.py:211
  5.6 0.2 reshape_squeeze.7
  5.8 1.3 %collective-permute-start.1 = (bf16[9,4,5120]{2,1,0:T(4,128)(2,1)S(1)}, bf16[9,4,5120]{2,1,0:T(4,128)(2,1)S(1)}, u32[]{:S(2)}, u32[]{:S(2)}) collective-permute-start(bf16[9,4,5120]{2,1,0:T(4,128)(2,1)S(1)} %reshape_squeeze.7), channel_id=1, source_target_pairs={{4,0},{8,4},{12,8},{16,12},{20,16},{24,20},{28,24},{5,1},{9,5},{13... | collective-permute-start | bytes 1105928 | tf_op jit(solution)/shard_map/ppermute | solution.py:212
  7.2 0.1 copy.23
  7.3 0.1 eq.17
  7.5 0.1 pad.16.clone
  7.6 13.2 %collective-permute-done.low_ref = bf16[9,4,5120]{2,1,0:T(4,128)(2,1)S(1)} collective-permute-done((bf16[9,4,5120]{2,1,0:T(4,128)(2,1)S(1)}, bf16[9,4,5120]{2,1,0:T(4,128)(2,1)S(1)}, u32[]{:S(2)}, u32[]{:S(2)}) %collective-permute-start) | collective-permute-done | bytes 368672 | tf_op jit(solution)/shard_map/ppermute | solution.py:211
  20.8 0.0 copy-start.8
  20.8 0.0 copy-start.7
  20.8 6.0 %shard_map.163 = bf16[3,16,5120]{2,1,0:T(8,128)(2,1)S(1)} custom-call(bf16[9,4,5120]{2,1,0:T(4,128)(2,1)S(1)} %collective-permute-done.low_ref, bf16[3,16,5120]{2,1,0:T(8,128)(2,1)S(1)} %bitcast.61, bf16[9,4,5120]{2,1,0:T(4,128)(2,1)S(1)} %collective-permute-done.1.high_ref, s32[16,5120]{1,0:T(8,128)S(1)} %bitcast.64, bf16[4,16,5120]{2,1,0:T(8,128)(2,1)S(1)} %bitcast.63), custom_call_target="tpu_custom_call" | custom-call | tf_op jit(solution)/shard_map/pallas_call | solution.py:78
  26.8 0.1 bitcast_convert_fusion
  26.9 0.1 subtract_convert_fusion.3
  27.0 0.4 fusion.26
  27.4 0.4 fusion.25
  27.9 1.1 %copy-done.4 = bf16[2,384,2560]{2,1,0:T(8,128)(2,1)S(1)} copy-done((bf16[2,384,2560]{2,1,0:T(8,128)(2,1)S(1)}, bf16[2,384,2560]{2,1,0:T(8,128)(2,1)}, u32[]{:S(2)}) %copy-start.4) | copy-done | bytes 3932184
  28.9 1.2 %fusion.24 = bf16[2,384,48]{1,2,0:T(8,128)(2,1)S(1)} fusion(bf16[2,384,2560]{2,1,0:T(8,128)(2,1)S(1)} %copy-done.4, bf16[48,1280]{1,0:T(8,128)(2,1)S(1)} %get-tuple-element.10, bf16[48,1280]{1,0:T(8,128)(2,1)S(1)} %get-tuple-element.9), kind=kOutput, calls=%fused_computation.22 | convolution fusion | flops 189272064 | bytes 4251648 | tf_op jit(solution)/shard_map/dot_general | solution.py:223
  30.2 0.1 pad_maximum_fusion.1
  30.3 0.6 fusion.21
  30.9 0.6 fusion.18
  31.5 0.1 maximum_maximum_fusion
  31.6 0.8 %copy.24 = bf16[768,128]{1,0:T(8,128)(2,1)} copy(bf16[768,128]{0,1:T(8,128)(2,1)S(1)} %maximum_maximum_fusion) | data formatting | bytes 393216 | tf_op jit(solution)/shard_map/concatenate | solution.py:233
  32.5 8.0 %all-to-all-start = ((bf16[32,24,128]{2,1,0:T(8,128)(2,1)}), bf16[32,24,128]{2,1,0:T(8,128)(2,1)S(1)}, u32[]{:S(2)}, u32[]{:S(2)}) async-start(bf16[32,24,128]{2,1,0:T(8,128)(2,1)} %bitcast.14), calls=%async_computation | async-start | bytes 393216 | tf_op jit(solution)/shard_map/all_to_all | solution.py:241
  40.5 0.1 dynamic_slice.3.pair_ref
  40.6 0.1 fusion.45
  40.7 9.0 %all-to-all-done.in_ref = bf16[32,24,128]{2,1,0:T(8,128)(2,1)S(1)} async-done(((bf16[32,24,128]{2,1,0:T(8,128)(2,1)}), bf16[32,24,128]{2,1,0:T(8,128)(2,1)S(1)}, u32[]{:S(2)}, u32[]{:S(2)}) %all-to-all-start) | async-done | bytes 196640 | tf_op jit(solution)/shard_map/all_to_all | solution.py:241
  49.7 5.8 %shard_map.164 = bf16[12,64,128]{2,1,0:T(8,128)(2,1)S(1)} custom-call(s32[12]{0:T(128)S(1)} %dynamic_slice.3.pair_ref, f32[16,1024]{1,0:T(8,128)S(1)} %get-tuple-element.14.table_ref, f32[16,1024]{1,0:T(8,128)S(1)} %get-tuple-element.13.shifted_ref, bf16[12,769,128]{2,1,0:T(8,128)(2,1)S(1)} %copy-done.1, bf16[32,24,128]{2,1,0:T(8,128)(2,1)S(1)} %all-to-all-done.in_ref), custom_call_target="tpu_custom_call" | custom-call | tf_op jit(solution)/shard_map/pallas_call | solution.py:170
  55.5 0.1 copy.31
  55.6 0.7 %reshape.83 = bf16[12,2,4,1,6,8,16]{6,5,2,4,1,0,3:T(8,128)(2,1)S(1)} reshape(bf16[12,2,4,6,128]{4,2,3,1,0:T(4,128)(2,1)S(1)} %copy.31) | data formatting | bytes 294912 | tf_op jit(solution)/shard_map/reshape | solution.py:247
  56.3 0.0 copy-start.16
  56.3 0.5 copy.26
  56.8 0.0 copy-start.11
  56.9 0.8 %all_to_all.16 = bf16[32,24,96]{2,1,0:T(8,128)(2,1)S(1)} reshape(bf16[8,4,12,2,6,1,16]{6,4,3,2,1,0,5:T(8,128)(2,1)S(1)} %copy.26) | data formatting | bytes 294912 | tf_op jit(solution)/shard_map/all_to_all | solution.py:251
  57.7 11.4 %all_to_all.21 = bf16[32,24,96]{2,1,0:T(8,128)(2,1)S(1)} all-to-all(bf16[32,24,96]{2,1,0:T(8,128)(2,1)S(1)} %all_to_all.16), channel_id=1, replica_groups=mesh['lat'=8,'lev'=4] {'lat','lev'}, dimensions={0} | all-to-all | bytes 294912 | tf_op jit(solution)/shard_map/all_to_all | solution.py:251
  69.1 0.5 fusion.15
  69.6 0.2 fusion.37
  69.8 0.0 copy-start.6
  69.9 0.2 fusion.40
  70.1 0.6 copy-done.5
  70.6 0.4 fusion.34
  71.1 0.0 copy-done.9
  71.1 0.3 convolution_add_fusion.1
  71.4 0.2 copy-done.6
  71.6 0.4 convolution_add_fusion
  72.0 0.2 copy-done.12
  72.2 0.2 add_convert_fusion.1
  72.5 0.8 %pad_maximum_fusion = bf16[3,1,16,5120]{3,2,1,0:T(8,128)(2,1)} fusion(bf16[3,1,16,1280]{3,2,1,0:T(8,128)(2,1)S(1)} %bitcast.68, bf16[3,1,16,1280]{3,2,1,0:T(8,128)(2,1)S(1)} %bitcast.67, bf16[3,1,16,1280]{3,2,1,0:T(8,128)(2,1)S(1)} %bitcast.69, bf16[3,1,16,1280]{3,2,1,0:T(8,128)(2,1)S(1)} %bitcast.66), kind=kLoop, calls=%fused_computation.27 | loop fusion | flops 1966080 | bytes 983040 | tf_op jit(solution)/shard_map/concatenate | solution.py:271
  (31 shorter events, 0.1 us)
Async XLA Ops:
  0.0 20.7 %copy-start = (bf16[3,1,16,5120]{3,2,1,0:T(8,128)(2,1)S(1)}, bf16[3,1,16,5120]{3,2,1,0:T(8,128)(2,1)}, u32[]{:S(2)}) copy-start(bf16[3,1,16,5120]{3,2,1,0:T(8,128)(2,1)} %param.17) | copy-start | bytes 1474564
  0.0 7.1 %copy-start.14 = (s32[384]{0:T(512)S(1)}, s32[384]{0:T(512)}, u32[]{:S(2)}) copy-start(s32[384]{0:T(512)} %param.20) | copy-start | bytes 4612
  0.0 20.7 %copy-start.2 = (bf16[4,1,16,5120]{3,2,1,0:T(8,128)(2,1)S(1)}, bf16[4,1,16,5120]{3,2,1,0:T(8,128)(2,1)}, u32[]{:S(2)}) copy-start(bf16[4,1,16,5120]{3,2,1,0:T(8,128)(2,1)} %param.19) | copy-start | bytes 1966084
  0.0 20.7 %copy-start.3 = (s32[1,16,5120]{2,1,0:T(8,128)S(1)}, s32[1,16,5120]{2,1,0:T(8,128)}, u32[]{:S(2)}) copy-start(s32[1,16,5120]{2,1,0:T(8,128)} %param.18) | copy-start | bytes 983044
  1.6 19.1 %collective-permute-start = (bf16[9,4,5120]{2,1,0:T(4,128)(2,1)S(1)}, bf16[9,4,5120]{2,1,0:T(4,128)(2,1)S(1)}, u32[]{:S(2)}, u32[]{:S(2)}) collective-permute-start(bf16[9,4,5120]{2,1,0:T(4,128)(2,1)S(1)} %reshape_squeeze.6), channel_id=1, source_target_pairs={{0,4},{4,8},{8,12},{12,16},{16,20},{20,24},{24,28},{1,5},{5,9},{9,... | collective-permute-start | bytes 1105928 | tf_op jit(solution)/shard_map/ppermute | solution.py:211
  5.8 14.9 %collective-permute-start.1 = (bf16[9,4,5120]{2,1,0:T(4,128)(2,1)S(1)}, bf16[9,4,5120]{2,1,0:T(4,128)(2,1)S(1)}, u32[]{:S(2)}, u32[]{:S(2)}) collective-permute-start(bf16[9,4,5120]{2,1,0:T(4,128)(2,1)S(1)} %reshape_squeeze.7), channel_id=1, source_target_pairs={{4,0},{8,4},{12,8},{16,12},{20,16},{24,20},{28,24},{5,1},{9,5},{13... | collective-permute-start | bytes 1105928 | tf_op jit(solution)/shard_map/ppermute | solution.py:212
  20.8 6.2 %copy-start.8 = (bf16[2,192,1280]{2,1,0:T(8,128)(2,1)S(1)}, bf16[2,192,1280]{2,1,0:T(8,128)(2,1)}, u32[]{:S(2)}) copy-start(bf16[2,192,1280]{2,1,0:T(8,128)(2,1)} %constant.47.clone) | copy-start | bytes 2949124
  20.8 6.7 %copy-start.7 = (bf16[2,192,1280]{2,1,0:T(8,128)(2,1)S(1)}, bf16[2,192,1280]{2,1,0:T(8,128)(2,1)}, u32[]{:S(2)}) copy-start(bf16[2,192,1280]{2,1,0:T(8,128)(2,1)} %constant.46.clone) | copy-start | bytes 2949124
  26.8 2.1 %copy-start.4 = (bf16[2,384,2560]{2,1,0:T(8,128)(2,1)S(1)}, bf16[2,384,2560]{2,1,0:T(8,128)(2,1)}, u32[]{:S(2)}) copy-start(bf16[2,384,2560]{2,1,0:T(8,128)(2,1)} %constant.48.clone) | copy-start | bytes 11796484
  28.9 1.4 %copy-start.15 = (s32[768]{0:T(1024)S(1)}, s32[768]{0:T(1024)}, u32[]{:S(2)}) copy-start(s32[768]{0:T(1024)} %constant.65) | copy-start | bytes 9220
  30.2 10.4 %copy-start.13 = (f32[768,4,4]{0,2,1:T(4,128)S(1)}, f32[768,4,4]{0,2,1:T(4,128)}, u32[]{:S(2)}) copy-start(f32[768,4,4]{0,2,1:T(4,128)} %param.22) | copy-start | bytes 147460
  30.2 19.5 %copy-start.1 = (bf16[12,769,128]{2,1,0:T(8,128)(2,1)S(1)}, bf16[12,769,128]{2,1,0:T(8,128)(2,1)}, u32[]{:S(2)}) copy-start(bf16[12,769,128]{2,1,0:T(8,128)(2,1)} %leg_ref.1) | copy-start | bytes 7087108
  32.5 17.3 %all-to-all-start = ((bf16[32,24,128]{2,1,0:T(8,128)(2,1)}), bf16[32,24,128]{2,1,0:T(8,128)(2,1)S(1)}, u32[]{:S(2)}, u32[]{:S(2)}) async-start(bf16[32,24,128]{2,1,0:T(8,128)(2,1)} %bitcast.14), calls=%async_computation | async-start | bytes 393216 | tf_op jit(solution)/shard_map/all_to_all | solution.py:241
  56.3 12.8 %copy-start.16 = (bf16[768]{0:T(1024)(128)(2,1)S(1)}, bf16[768]{0:T(1024)(128)(2,1)}, u32[]{:S(2)}) copy-start(bf16[768]{0:T(1024)(128)(2,1)} %constant.104) | copy-start | bytes 4612
  56.8 12.7 %copy-start.11 = (bf16[192,1280]{1,0:T(8,128)(2,1)S(1)}, bf16[192,1280]{1,0:T(8,128)(2,1)}, u32[]{:S(2)}) copy-start(bf16[192,1280]{1,0:T(8,128)(2,1)} %constant.53.clone) | copy-start | bytes 1474564
  57.7 12.2 %copy-start.10 = (bf16[192,1280]{1,0:T(8,128)(2,1)S(1)}, bf16[192,1280]{1,0:T(8,128)(2,1)}, u32[]{:S(2)}) copy-start(bf16[192,1280]{1,0:T(8,128)(2,1)} %constant.51.clone) | copy-start | bytes 1474564
  69.1 1.5 %copy-start.5 = (bf16[384,2560]{1,0:T(8,128)(2,1)S(1)}, bf16[384,2560]{1,0:T(8,128)(2,1)}, u32[]{:S(2)}) copy-start(bf16[384,2560]{1,0:T(8,128)(2,1)} %constant.55.clone) | copy-start | bytes 5898244
  69.6 1.5 %copy-start.9 = (bf16[192,1280]{1,0:T(8,128)(2,1)S(1)}, bf16[192,1280]{1,0:T(8,128)(2,1)}, u32[]{:S(2)}) copy-start(bf16[192,1280]{1,0:T(8,128)(2,1)} %constant.54.clone) | copy-start | bytes 1474564
  69.8 1.7 %copy-start.6 = (bf16[384,2560]{1,0:T(8,128)(2,1)S(1)}, bf16[384,2560]{1,0:T(8,128)(2,1)}, u32[]{:S(2)}) copy-start(bf16[384,2560]{1,0:T(8,128)(2,1)} %constant.56.clone) | copy-start | bytes 5898244
  71.1 1.2 %copy-start.12 = (bf16[192,1280]{1,0:T(8,128)(2,1)S(1)}, bf16[192,1280]{1,0:T(8,128)(2,1)}, u32[]{:S(2)}) copy-start(bf16[192,1280]{1,0:T(8,128)(2,1)} %constant.52.clone) | copy-start | bytes 1474564

commit v3 on v2

--- a/solution.py
+++ b/solution.py
@@ -92,6 +92,17 @@
     )(low, mid, high, offset, weights)
 
 
+def exchange(parts, tile):
+    for bit in (1, 2, 4):
+        low_side = (tile & bit) == 0
+        step = bit * (LANES // GROUP)
+        for i in range(GROUP):
+            if i & bit == 0:
+                a, b = parts[i], parts[i + bit]
+                parts[i] = jnp.where(low_side, a, pltpu.roll(b, step, 1))
+                parts[i + bit] = jnp.where(low_side, pltpu.roll(a, LANES - step, 1), b)
+
+
 def spectral_kernel(wave_count, level_count, pair_ref, table_ref, shifted_ref, leg_ref, in_ref, out_ref, lines):
     pair = pair_ref[pl.program_id(0)]
     slots = leg_ref.shape[1]
@@ -108,16 +119,7 @@
                     in_ref[(g * GROUP + i) * level_count + level].astype(jnp.float32)
                     for i in range(GROUP)
                 ]
-                for bit in (1, 2, 4):
-                    low_side = (tile & bit) == 0
-                    step = bit * (LANES // GROUP)
-                    for i in range(GROUP):
-                        if i & bit == 0:
-                            a, b = parts[i], parts[i + bit]
-                            parts[i] = jnp.where(low_side, a, pltpu.roll(b, step, 1))
-                            parts[i + bit] = jnp.where(
-                                low_side, pltpu.roll(a, LANES - step, 1), b
-                            )
+                exchange(parts, tile)
                 for i in range(GROUP):
                     first = (level * GROUP + i) * local_rows
                     lines[g, first : first + local_rows, :] = parts[i]
@@ -155,13 +157,31 @@
     returned = jnp.dot(
         placed.astype(jnp.bfloat16), legendre, preferred_element_type=jnp.float32
     )
-    out_ref[0] = returned.astype(out_ref.dtype)
+    for which in range(2):
+        start = 2 * pl.program_id(0) + which
+        for g in range(lines.shape[0]):
+            lines[g, pl.ds(start, half, stride=local_rows), :] = returned[
+                which * half : (which + 1) * half, g * LANES : (g + 1) * LANES
+            ]
+
+    @pl.when(pl.program_id(0) == pl.num_programs(0) - 1)
+    def _():
+        tile = lax.broadcasted_iota(jnp.int32, (local_rows, LANES), 1) // (LANES // GROUP)
+        for g in range(lines.shape[0]):
+            for level in range(level_count):
+                parts = []
+                for i in range(GROUP):
+                    first = (level * GROUP + i) * local_rows
+                    parts.append(lines[g, first : first + local_rows, :])
+                exchange(parts, tile)
+                for i in range(GROUP):
+                    holder = (g * GROUP + i) * level_count + level
+                    out_ref[holder] = parts[i].astype(out_ref.dtype)
 
 
 def spectral(pair_here, helmholtz, legendre, moved):
     pair_local, slot_count, lat_total = legendre.shape
     wave_count, level_count, _ = helmholtz.shape
-    rows = 2 * level_count * GROUP
     span = -(-slot_count // 256) * 256
     flat = helmholtz.reshape(wave_count, level_count * level_count).T
     table = jnp.pad(flat, ((0, 0), (0, span - wave_count)))
@@ -178,14 +198,14 @@
                 pl.BlockSpec((1, slot_count, lat_total), lambda i, pair: (i, 0, 0)),
                 pl.BlockSpec(moved.shape, lambda i, pair: (0, 0, 0)),
             ],
-            out_specs=pl.BlockSpec((1, rows, lat_total), lambda i, pair: (i, 0, 0)),
+            out_specs=pl.BlockSpec(moved.shape, lambda i, pair: (0, 0, 0)),
             scratch_shapes=[
                 pltpu.VMEM(
                     (lat_total // LANES, level_count * GROUP * moved.shape[1], LANES), jnp.float32
                 )
             ],
         ),
-        out_shape=jax.ShapeDtypeStruct((pair_local, rows, lat_total), moved.dtype),
+        out_shape=jax.ShapeDtypeStruct(moved.shape, moved.dtype),
         compiler_params=pltpu.CompilerParams(vmem_limit_bytes=32 * 1024 * 1024),
     )(pair_here, table, shifted, legendre, moved)
 
@@ -243,11 +263,7 @@
     holder = lax.axis_index("lat") * lev_count + lax.axis_index("lev")
     pair_here = lax.dynamic_slice_in_dim(pair_order, holder * pair_local, pair_local)
     returned = spectral(pair_here, helmholtz, legendre, moved)
-    returned = returned.reshape(pair_local, 2, level_count, GROUP, lat_total)[:, :, :, : 2 * fields]
-    returned = returned.reshape(
-        pair_local, 2, lev_count, lev_local, 2 * fields, lat_count, row_count
-    )
-    outgoing = returned.transpose(5, 2, 0, 1, 4, 3, 6).reshape(pair_count * 2, 2 * local)
+    outgoing = returned.reshape(2 * pair_count, LANES)
     arrived = lax.all_to_all(outgoing, ("lat", "lev"), split_axis=0, concat_axis=0, tiled=True)
     gain = jnp.where(match, np.where(order == 0, 1.0, 2.0).astype(np.float32)[None, :], 0.0)
     natural = lax.dot_general(

time: 73.6 us -> 71.3 us (0.969)
  local copies, waits for them, and re-layouts: 7.39 us -> 4.81 us
    all_to_all x1 -> x0, local copies, waits for them, and re-layouts: 0.81 us -> none  [shards(): lax.all_to_all(outgoing, ('lat', 'lev'), split_axis=0, concat_axis=0, til...]
    reshape x1 -> x0, local copies, waits for them, and re-layouts: 0.74 us -> none  [shards(): returned.reshape(pair_local, 2, lev_count, lev_local, 2 * fields, lat_cou...]
    unnamed x35 -> x34, local copies, waits for them, and re-layouts: 2.2 us -> 1.68 us
where the time goes in v3:
time: 71.3 us; the launch traced here: 71 us
  waiting for transfers between devices  22.2 us (31%)
  starting transfers between devices  13.3 us (19%)
  Pallas kernels  12.1 us (17%)
  blocking collectives  11.4 us (16%)
  matrix products  5.62 us (8%)
  local copies, waits for them, and re-layouts  4.81 us (7%)
  other arithmetic  1.16 us (2%)
    ppermute x1, waiting for transfers between devices, shards(): lax.ppermute(grid_old[:, 0, row_count - HMAX:].reshape(groups), 'lat', fo...  13.2 us
    all_to_all x1, blocking collectives, shards(): lax.all_to_all(outgoing, ('lat', 'lev'), split_axis=0, concat_axis=0, til...  11.4 us
    all_to_all x1, waiting for transfers between devices, shards(): lax.all_to_all(sent, ('lat', 'lev'), split_axis=0, concat_axis=0, tiled=T...  9.04 us
    all_to_all x1, starting transfers between devices, shards(): lax.all_to_all(sent, ('lat', 'lev'), split_axis=0, concat_axis=0, tiled=T...  8.04 us
    pallas_call x1, Pallas kernels, spectral(): pl.pallas_call(functools.partial(spectral_kernel, wave_count, level_count...  6.1 us
    pallas_call x1, Pallas kernels, interpolate(): pl.pallas_call(interp_kernel, grid=(lon_count // width,), out_shape=jax.S...  6.03 us
    ppermute x1, starting transfers between devices, shards(): lax.ppermute(grid_old[:, 0, row_count - HMAX:].reshape(groups), 'lat', fo...  4 us
    dot_general x3, matrix products, project(): lax.dot_general(basis, part, (((2,), (1,)), ((), ())), preferred_element_...  2.08 us
  transfers between devices with their start and end apart: 3, of which 2 were waited for; matrix products, arithmetic and copies ran while one was open for 1% of the time, Pallas kernels for 0%

profile of v3, /device:TPU:1, one launch (start us, length us, event | category | flops | bytes accessed | tf_op | source)
XLA Modules:
  0.0 71.0 jit_solution(12927828193167011193)
XLA Ops:
  0.0 1.4 %fusion.44 = (bf16[3,1,12,5120]{3,2,1,0:T(8,128)(2,1)S(1)}, bf16[3,1,12,5120]{3,2,1,0:T(8,128)(2,1)S(1)}) fusion(bf16[3,1,16,5120]{3,2,1,0:T(8,128)(2,1)} %param.17), kind=kLoop, calls=%fused_computation.61 | loop fusion | bytes 1474560 | tf_op jit(solution)/shard_map/slice | solution.py:232
  1.4 0.2 reshape_squeeze.6
  1.6 4.0 %collective-permute-start = (bf16[9,4,5120]{2,1,0:T(4,128)(2,1)S(1)}, bf16[9,4,5120]{2,1,0:T(4,128)(2,1)S(1)}, u32[]{:S(2)}, u32[]{:S(2)}) collective-permute-start(bf16[9,4,5120]{2,1,0:T(4,128)(2,1)S(1)} %reshape_squeeze.6), channel_id=1, source_target_pairs={{0,4},{4,8},{8,12},{12,16},{16,20},{20,24},{24,28},{1,5},{5,9},{9,... | collective-permute-start | bytes 1105928 | tf_op jit(solution)/shard_map/ppermute | solution.py:231
  5.6 0.2 reshape_squeeze.7
  5.8 1.3 %collective-permute-start.1 = (bf16[9,4,5120]{2,1,0:T(4,128)(2,1)S(1)}, bf16[9,4,5120]{2,1,0:T(4,128)(2,1)S(1)}, u32[]{:S(2)}, u32[]{:S(2)}) collective-permute-start(bf16[9,4,5120]{2,1,0:T(4,128)(2,1)S(1)} %reshape_squeeze.7), channel_id=1, source_target_pairs={{4,0},{8,4},{12,8},{16,12},{20,16},{24,20},{28,24},{5,1},{9,5},{13... | collective-permute-start | bytes 1105928 | tf_op jit(solution)/shard_map/ppermute | solution.py:232
  7.2 0.1 copy.23
  7.3 0.1 eq.17
  7.5 0.1 pad.16.clone
  7.6 13.2 %collective-permute-done.low_ref = bf16[9,4,5120]{2,1,0:T(4,128)(2,1)S(1)} collective-permute-done((bf16[9,4,5120]{2,1,0:T(4,128)(2,1)S(1)}, bf16[9,4,5120]{2,1,0:T(4,128)(2,1)S(1)}, u32[]{:S(2)}, u32[]{:S(2)}) %collective-permute-start) | collective-permute-done | bytes 368672 | tf_op jit(solution)/shard_map/ppermute | solution.py:231
  20.8 0.0 copy-start.8
  20.8 0.0 copy-start.7
  20.8 6.0 %shard_map.163 = bf16[3,16,5120]{2,1,0:T(8,128)(2,1)S(1)} custom-call(bf16[9,4,5120]{2,1,0:T(4,128)(2,1)S(1)} %collective-permute-done.low_ref, bf16[3,16,5120]{2,1,0:T(8,128)(2,1)S(1)} %bitcast.54, bf16[9,4,5120]{2,1,0:T(4,128)(2,1)S(1)} %collective-permute-done.1.high_ref, s32[16,5120]{1,0:T(8,128)S(1)} %bitcast.56, bf16[4,16,5120]{2,1,0:T(8,128)(2,1)S(1)} %bitcast.55), custom_call_target="tpu_custom_call" | custom-call | tf_op jit(solution)/shard_map/pallas_call | solution.py:78
  26.8 0.0 copy-start.4
  26.8 0.1 bitcast_convert_fusion
  26.9 0.1 subtract_convert_fusion.3
  27.0 0.4 fusion.26
  27.4 0.4 fusion.25
  27.9 0.0 copy-start.15
  27.9 1.0 %copy-done.4 = bf16[2,384,2560]{2,1,0:T(8,128)(2,1)S(1)} copy-done((bf16[2,384,2560]{2,1,0:T(8,128)(2,1)S(1)}, bf16[2,384,2560]{2,1,0:T(8,128)(2,1)}, u32[]{:S(2)}) %copy-start.4) | copy-done | bytes 3932184
  28.9 1.2 %fusion.24 = bf16[2,384,48]{1,2,0:T(8,128)(2,1)S(1)} fusion(bf16[2,384,2560]{2,1,0:T(8,128)(2,1)S(1)} %copy-done.4, bf16[48,1280]{1,0:T(8,128)(2,1)S(1)} %get-tuple-element.10, bf16[48,1280]{1,0:T(8,128)(2,1)S(1)} %get-tuple-element.9), kind=kOutput, calls=%fused_computation.22 | convolution fusion | flops 189272064 | bytes 4251648 | tf_op jit(solution)/shard_map/dot_general | solution.py:243
  30.2 0.0 copy-start.13
  30.2 0.1 pad_maximum_fusion.1
  30.3 0.6 fusion.21
  30.9 0.6 fusion.18
  31.5 0.0 copy-start.16
  31.5 0.1 maximum_maximum_fusion
  31.6 0.8 %copy.24 = bf16[768,128]{1,0:T(8,128)(2,1)} copy(bf16[768,128]{0,1:T(8,128)(2,1)S(1)} %maximum_maximum_fusion) | data formatting | bytes 393216 | tf_op jit(solution)/shard_map/concatenate | solution.py:253
  32.5 8.0 %all-to-all-start = ((bf16[32,24,128]{2,1,0:T(8,128)(2,1)}), bf16[32,24,128]{2,1,0:T(8,128)(2,1)S(1)}, u32[]{:S(2)}, u32[]{:S(2)}) async-start(bf16[32,24,128]{2,1,0:T(8,128)(2,1)} %bitcast.14), calls=%async_computation | async-start | bytes 393216 | tf_op jit(solution)/shard_map/all_to_all | solution.py:261
  40.5 0.1 dynamic_slice.3.pair_ref
  40.6 0.1 fusion.45
  40.7 9.0 %all-to-all-done.in_ref = bf16[32,24,128]{2,1,0:T(8,128)(2,1)S(1)} async-done(((bf16[32,24,128]{2,1,0:T(8,128)(2,1)}), bf16[32,24,128]{2,1,0:T(8,128)(2,1)S(1)}, u32[]{:S(2)}, u32[]{:S(2)}) %all-to-all-start) | async-done | bytes 196640 | tf_op jit(solution)/shard_map/all_to_all | solution.py:261
  49.7 6.1 %shard_map.164 = bf16[32,24,128]{2,1,0:T(8,128)(2,1)S(1)} custom-call(s32[12]{0:T(128)S(1)} %dynamic_slice.3.pair_ref, f32[16,1024]{1,0:T(8,128)S(1)} %get-tuple-element.14.table_ref, f32[16,1024]{1,0:T(8,128)S(1)} %get-tuple-element.13.shifted_ref, bf16[12,769,128]{2,1,0:T(8,128)(2,1)S(1)} %copy-done.1, bf16[32,24,128]{2,1,0:T(8,128)(2,1)S(1)} %all-to-all-done.in_ref), custom_call_target="tpu_custom_call" | custom-call | tf_op jit(solution)/shard_map/pallas_call | solution.py:190
  55.8 0.0 copy-start.10
  55.9 0.0 copy-start.5
  55.9 11.4 %all_to_all.18 = bf16[32,24,128]{2,1,0:T(8,128)(2,1)S(1)} all-to-all(bf16[32,24,128]{2,1,0:T(8,128)(2,1)S(1)} %shard_map.164), channel_id=1, replica_groups=mesh['lat'=8,'lev'=4] {'lat','lev'}, dimensions={0} | all-to-all | bytes 393216 | tf_op jit(solution)/shard_map/all_to_all | solution.py:267
  67.3 0.5 fusion.15
  67.8 0.0 copy-start.9
  67.8 0.0 copy-start.6
  67.8 0.2 fusion.37
  68.0 0.2 fusion.40
  68.3 0.4 fusion.34
  68.7 0.1 copy-done.9
  68.8 0.3 convolution_add_fusion.1
  69.1 0.4 copy-done.6
  69.5 0.4 convolution_add_fusion
  69.9 0.0 copy-done.12
  70.0 0.2 add_convert_fusion.1
  70.2 0.8 %pad_maximum_fusion = bf16[3,1,16,5120]{3,2,1,0:T(8,128)(2,1)} fusion(bf16[3,1,16,1280]{3,2,1,0:T(8,128)(2,1)S(1)} %bitcast.59, bf16[3,1,16,1280]{3,2,1,0:T(8,128)(2,1)S(1)} %bitcast.58, bf16[3,1,16,1280]{3,2,1,0:T(8,128)(2,1)S(1)} %bitcast.60, bf16[3,1,16,1280]{3,2,1,0:T(8,128)(2,1)S(1)} %bitcast.57), kind=kLoop, calls=%fused_computation.27 | loop fusion | flops 1966080 | bytes 983040 | tf_op jit(solution)/shard_map/concatenate | solution.py:287
  (27 shorter events, 0.1 us)
Async XLA Ops:
  0.0 20.7 %copy-start = (bf16[3,1,16,5120]{3,2,1,0:T(8,128)(2,1)S(1)}, bf16[3,1,16,5120]{3,2,1,0:T(8,128)(2,1)}, u32[]{:S(2)}) copy-start(bf16[3,1,16,5120]{3,2,1,0:T(8,128)(2,1)} %param.17) | copy-start | bytes 1474564
  0.0 7.1 %copy-start.14 = (s32[384]{0:T(512)S(1)}, s32[384]{0:T(512)}, u32[]{:S(2)}) copy-start(s32[384]{0:T(512)} %param.20) | copy-start | bytes 4612
  0.0 20.7 %copy-start.2 = (bf16[4,1,16,5120]{3,2,1,0:T(8,128)(2,1)S(1)}, bf16[4,1,16,5120]{3,2,1,0:T(8,128)(2,1)}, u32[]{:S(2)}) copy-start(bf16[4,1,16,5120]{3,2,1,0:T(8,128)(2,1)} %param.19) | copy-start | bytes 1966084
  0.0 20.7 %copy-start.3 = (s32[1,16,5120]{2,1,0:T(8,128)S(1)}, s32[1,16,5120]{2,1,0:T(8,128)}, u32[]{:S(2)}) copy-start(s32[1,16,5120]{2,1,0:T(8,128)} %param.18) | copy-start | bytes 983044
  1.6 19.1 %collective-permute-start = (bf16[9,4,5120]{2,1,0:T(4,128)(2,1)S(1)}, bf16[9,4,5120]{2,1,0:T(4,128)(2,1)S(1)}, u32[]{:S(2)}, u32[]{:S(2)}) collective-permute-start(bf16[9,4,5120]{2,1,0:T(4,128)(2,1)S(1)} %reshape_squeeze.6), channel_id=1, source_target_pairs={{0,4},{4,8},{8,12},{12,16},{16,20},{20,24},{24,28},{1,5},{5,9},{9,... | collective-permute-start | bytes 1105928 | tf_op jit(solution)/shard_map/ppermute | solution.py:231
  5.8 14.9 %collective-permute-start.1 = (bf16[9,4,5120]{2,1,0:T(4,128)(2,1)S(1)}, bf16[9,4,5120]{2,1,0:T(4,128)(2,1)S(1)}, u32[]{:S(2)}, u32[]{:S(2)}) collective-permute-start(bf16[9,4,5120]{2,1,0:T(4,128)(2,1)S(1)} %reshape_squeeze.7), channel_id=1, source_target_pairs={{4,0},{8,4},{12,8},{16,12},{20,16},{24,20},{28,24},{5,1},{9,5},{13... | collective-permute-start | bytes 1105928 | tf_op jit(solution)/shard_map/ppermute | solution.py:232
  20.8 6.2 %copy-start.8 = (bf16[2,192,1280]{2,1,0:T(8,128)(2,1)S(1)}, bf16[2,192,1280]{2,1,0:T(8,128)(2,1)}, u32[]{:S(2)}) copy-start(bf16[2,192,1280]{2,1,0:T(8,128)(2,1)} %constant.47.clone) | copy-start | bytes 2949124
  20.8 6.7 %copy-start.7 = (bf16[2,192,1280]{2,1,0:T(8,128)(2,1)S(1)}, bf16[2,192,1280]{2,1,0:T(8,128)(2,1)}, u32[]{:S(2)}) copy-start(bf16[2,192,1280]{2,1,0:T(8,128)(2,1)} %constant.46.clone) | copy-start | bytes 2949124
  26.8 2.1 %copy-start.4 = (bf16[2,384,2560]{2,1,0:T(8,128)(2,1)S(1)}, bf16[2,384,2560]{2,1,0:T(8,128)(2,1)}, u32[]{:S(2)}) copy-start(bf16[2,384,2560]{2,1,0:T(8,128)(2,1)} %constant.48.clone) | copy-start | bytes 11796484
  27.9 2.4 %copy-start.15 = (s32[768]{0:T(1024)S(1)}, s32[768]{0:T(1024)}, u32[]{:S(2)}) copy-start(s32[768]{0:T(1024)} %constant.65) | copy-start | bytes 9220
  30.2 10.4 %copy-start.13 = (f32[768,4,4]{0,2,1:T(4,128)S(1)}, f32[768,4,4]{0,2,1:T(4,128)}, u32[]{:S(2)}) copy-start(f32[768,4,4]{0,2,1:T(4,128)} %param.22) | copy-start | bytes 147460
  30.2 19.6 %copy-start.1 = (bf16[12,769,128]{2,1,0:T(8,128)(2,1)S(1)}, bf16[12,769,128]{2,1,0:T(8,128)(2,1)}, u32[]{:S(2)}) copy-start(bf16[12,769,128]{2,1,0:T(8,128)(2,1)} %leg_ref.1) | copy-start | bytes 7087108
  31.5 35.8 %copy-start.16 = (bf16[768]{0:T(1024)(128)(2,1)S(1)}, bf16[768]{0:T(1024)(128)(2,1)}, u32[]{:S(2)}) copy-start(bf16[768]{0:T(1024)(128)(2,1)} %constant.104) | copy-start | bytes 4612
  32.5 17.3 %all-to-all-start = ((bf16[32,24,128]{2,1,0:T(8,128)(2,1)}), bf16[32,24,128]{2,1,0:T(8,128)(2,1)S(1)}, u32[]{:S(2)}, u32[]{:S(2)}) async-start(bf16[32,24,128]{2,1,0:T(8,128)(2,1)} %bitcast.14), calls=%async_computation | async-start | bytes 393216 | tf_op jit(solution)/shard_map/all_to_all | solution.py:261
  49.7 18.0 %copy-start.11 = (bf16[192,1280]{1,0:T(8,128)(2,1)S(1)}, bf16[192,1280]{1,0:T(8,128)(2,1)}, u32[]{:S(2)}) copy-start(bf16[192,1280]{1,0:T(8,128)(2,1)} %constant.53.clone) | copy-start | bytes 1474564
  55.8 12.2 %copy-start.10 = (bf16[192,1280]{1,0:T(8,128)(2,1)S(1)}, bf16[192,1280]{1,0:T(8,128)(2,1)}, u32[]{:S(2)}) copy-start(bf16[192,1280]{1,0:T(8,128)(2,1)} %constant.51.clone) | copy-start | bytes 1474564
  55.9 12.4 %copy-start.5 = (bf16[384,2560]{1,0:T(8,128)(2,1)S(1)}, bf16[384,2560]{1,0:T(8,128)(2,1)}, u32[]{:S(2)}) copy-start(bf16[384,2560]{1,0:T(8,128)(2,1)} %constant.55.clone) | copy-start | bytes 5898244
  67.8 1.0 %copy-start.9 = (bf16[192,1280]{1,0:T(8,128)(2,1)S(1)}, bf16[192,1280]{1,0:T(8,128)(2,1)}, u32[]{:S(2)}) copy-start(bf16[192,1280]{1,0:T(8,128)(2,1)} %constant.54.clone) | copy-start | bytes 1474564
  67.8 1.7 %copy-start.6 = (bf16[384,2560]{1,0:T(8,128)(2,1)S(1)}, bf16[384,2560]{1,0:T(8,128)(2,1)}, u32[]{:S(2)}) copy-start(bf16[384,2560]{1,0:T(8,128)(2,1)} %constant.56.clone) | copy-start | bytes 5898244
  68.8 1.2 %copy-start.12 = (bf16[192,1280]{1,0:T(8,128)(2,1)S(1)}, bf16[192,1280]{1,0:T(8,128)(2,1)}, u32[]{:S(2)}) copy-start(bf16[192,1280]{1,0:T(8,128)(2,1)} %constant.52.clone) | copy-start | bytes 1474564

commit v4 on v3

--- a/solution.py
+++ b/solution.py
@@ -51,20 +51,21 @@
         offset = offset_ref[:, here]
         weights = [weight_ref[k, :, here].astype(jnp.float32) for k in range(4)]
         totals = [jnp.zeros((rows, LANES), jnp.float32) for _ in range(fields)]
-        picks = [offset == start for start in range(-HMAX, HMAX - 2)]
+        picks = {}
         for shift in range(-HMAX, HMAX + 1):
             coefficient = jnp.zeros((rows, LANES), jnp.float32)
+            picks[shift] = offset == shift
             for k in range(4):
                 start = shift - k
                 if -HMAX <= start < HMAX - 2:
-                    coefficient = jnp.where(picks[start + HMAX], weights[k], coefficient)
+                    coefficient = jnp.where(picks[start], weights[k], coefficient)
             for f in range(fields):
                 totals[f] = totals[f] + coefficient * wide[f, pl.ds(rows + shift, rows), here]
         for f in range(fields):
             out_ref[f, :, here] = totals[f].astype(out_ref.dtype)
         return carry
 
-    lax.fori_loop(0, width // LANES, chunk, 0)
+    lax.fori_loop(0, width // LANES, chunk, 0, unroll=2)
 
 
 def interpolate(low, mid, high, offset, weights):

time: 71.3 us -> 71 us (level)
  no operation moved by 1% of the time
where the time goes in v4:
time: 71 us; the launch traced here: 70.7 us
  waiting for transfers between devices  22.2 us (31%)
  starting transfers between devices  13.3 us (19%)
  Pallas kernels  11.8 us (17%)
  blocking collectives  11.4 us (16%)
  matrix products  5.62 us (8%)
  local copies, waits for them, and re-layouts  4.81 us (7%)
  other arithmetic  1.16 us (2%)
    ppermute x1, waiting for transfers between devices, shards(): lax.ppermute(grid_old[:, 0, row_count - HMAX:].reshape(groups), 'lat', fo...  13.2 us
    all_to_all x1, blocking collectives, shards(): lax.all_to_all(outgoing, ('lat', 'lev'), split_axis=0, concat_axis=0, til...  11.4 us
    all_to_all x1, waiting for transfers between devices, shards(): lax.all_to_all(sent, ('lat', 'lev'), split_axis=0, concat_axis=0, tiled=T...  9.04 us
    all_to_all x1, starting transfers between devices, shards(): lax.all_to_all(sent, ('lat', 'lev'), split_axis=0, concat_axis=0, tiled=T...  8.04 us
    pallas_call x1, Pallas kernels, spectral(): pl.pallas_call(functools.partial(spectral_kernel, wave_count, level_count...  6.11 us
    pallas_call x1, Pallas kernels, interpolate(): pl.pallas_call(interp_kernel, grid=(lon_count // width,), out_shape=jax.S...  5.72 us
    ppermute x1, starting transfers between devices, shards(): lax.ppermute(grid_old[:, 0, row_count - HMAX:].reshape(groups), 'lat', fo...  4 us
    dot_general x3, matrix products, project(): lax.dot_general(basis, part, (((2,), (1,)), ((), ())), preferred_element_...  2.08 us
  transfers between devices with their start and end apart: 3, of which 2 were waited for; matrix products, arithmetic and copies ran while one was open for 1% of the time, Pallas kernels for 0%

profile of v4, /device:TPU:1, one launch (start us, length us, event | category | flops | bytes accessed | tf_op | source)
XLA Modules:
  0.0 70.7 jit_solution(9105843285100118209)
XLA Ops:
  0.0 1.4 %fusion.44 = (bf16[3,1,12,5120]{3,2,1,0:T(8,128)(2,1)S(1)}, bf16[3,1,12,5120]{3,2,1,0:T(8,128)(2,1)S(1)}) fusion(bf16[3,1,16,5120]{3,2,1,0:T(8,128)(2,1)} %param.17), kind=kLoop, calls=%fused_computation.61 | loop fusion | bytes 1474560 | tf_op jit(solution)/shard_map/slice | solution.py:233
  1.4 0.2 reshape_squeeze.6
  1.6 4.0 %collective-permute-start = (bf16[9,4,5120]{2,1,0:T(4,128)(2,1)S(1)}, bf16[9,4,5120]{2,1,0:T(4,128)(2,1)S(1)}, u32[]{:S(2)}, u32[]{:S(2)}) collective-permute-start(bf16[9,4,5120]{2,1,0:T(4,128)(2,1)S(1)} %reshape_squeeze.6), channel_id=1, source_target_pairs={{0,4},{4,8},{8,12},{12,16},{16,20},{20,24},{24,28},{1,5},{5,9},{9,... | collective-permute-start | bytes 1105928 | tf_op jit(solution)/shard_map/ppermute | solution.py:232
  5.6 0.2 reshape_squeeze.7
  5.8 1.3 %collective-permute-start.1 = (bf16[9,4,5120]{2,1,0:T(4,128)(2,1)S(1)}, bf16[9,4,5120]{2,1,0:T(4,128)(2,1)S(1)}, u32[]{:S(2)}, u32[]{:S(2)}) collective-permute-start(bf16[9,4,5120]{2,1,0:T(4,128)(2,1)S(1)} %reshape_squeeze.7), channel_id=1, source_target_pairs={{4,0},{8,4},{12,8},{16,12},{20,16},{24,20},{28,24},{5,1},{9,5},{13... | collective-permute-start | bytes 1105928 | tf_op jit(solution)/shard_map/ppermute | solution.py:233
  7.2 0.1 copy.23
  7.3 0.1 eq.17
  7.5 0.1 pad.16.clone
  7.6 13.2 %collective-permute-done.low_ref = bf16[9,4,5120]{2,1,0:T(4,128)(2,1)S(1)} collective-permute-done((bf16[9,4,5120]{2,1,0:T(4,128)(2,1)S(1)}, bf16[9,4,5120]{2,1,0:T(4,128)(2,1)S(1)}, u32[]{:S(2)}, u32[]{:S(2)}) %collective-permute-start) | collective-permute-done | bytes 368672 | tf_op jit(solution)/shard_map/ppermute | solution.py:232
  20.8 0.0 copy-start.8
  20.8 0.0 copy-start.7
  20.8 5.7 %shard_map.163 = bf16[3,16,5120]{2,1,0:T(8,128)(2,1)S(1)} custom-call(bf16[9,4,5120]{2,1,0:T(4,128)(2,1)S(1)} %collective-permute-done.low_ref, bf16[3,16,5120]{2,1,0:T(8,128)(2,1)S(1)} %bitcast.54, bf16[9,4,5120]{2,1,0:T(4,128)(2,1)S(1)} %collective-permute-done.1.high_ref, s32[16,5120]{1,0:T(8,128)S(1)} %bitcast.56, bf16[4,16,5120]{2,1,0:T(8,128)(2,1)S(1)} %bitcast.55), custom_call_target="tpu_custom_call" | custom-call | tf_op jit(solution)/shard_map/pallas_call | solution.py:79
  26.5 0.0 copy-start.4
  26.5 0.1 bitcast_convert_fusion
  26.6 0.1 subtract_convert_fusion.3
  26.7 0.4 fusion.26
  27.1 0.4 fusion.25
  27.6 0.0 copy-start.15
  27.6 1.0 %copy-done.4 = bf16[2,384,2560]{2,1,0:T(8,128)(2,1)S(1)} copy-done((bf16[2,384,2560]{2,1,0:T(8,128)(2,1)S(1)}, bf16[2,384,2560]{2,1,0:T(8,128)(2,1)}, u32[]{:S(2)}) %copy-start.4) | copy-done | bytes 3932184
  28.6 1.2 %fusion.24 = bf16[2,384,48]{1,2,0:T(8,128)(2,1)S(1)} fusion(bf16[2,384,2560]{2,1,0:T(8,128)(2,1)S(1)} %copy-done.4, bf16[48,1280]{1,0:T(8,128)(2,1)S(1)} %get-tuple-element.10, bf16[48,1280]{1,0:T(8,128)(2,1)S(1)} %get-tuple-element.9), kind=kOutput, calls=%fused_computation.22 | convolution fusion | flops 189272064 | bytes 4251648 | tf_op jit(solution)/shard_map/dot_general | solution.py:244
  29.9 0.0 copy-start.1
  29.9 0.1 pad_maximum_fusion.1
  30.0 0.6 fusion.21
  30.6 0.6 fusion.18
  31.2 0.0 copy-start.16
  31.2 0.1 maximum_maximum_fusion
  31.3 0.8 %copy.24 = bf16[768,128]{1,0:T(8,128)(2,1)} copy(bf16[768,128]{0,1:T(8,128)(2,1)S(1)} %maximum_maximum_fusion) | data formatting | bytes 393216 | tf_op jit(solution)/shard_map/concatenate | solution.py:254
  32.1 8.0 %all-to-all-start = ((bf16[32,24,128]{2,1,0:T(8,128)(2,1)}), bf16[32,24,128]{2,1,0:T(8,128)(2,1)S(1)}, u32[]{:S(2)}, u32[]{:S(2)}) async-start(bf16[32,24,128]{2,1,0:T(8,128)(2,1)} %bitcast.14), calls=%async_computation | async-start | bytes 393216 | tf_op jit(solution)/shard_map/all_to_all | solution.py:262
  40.2 0.1 dynamic_slice.3.pair_ref
  40.3 0.1 fusion.45
  40.4 9.0 %all-to-all-done.in_ref = bf16[32,24,128]{2,1,0:T(8,128)(2,1)S(1)} async-done(((bf16[32,24,128]{2,1,0:T(8,128)(2,1)}), bf16[32,24,128]{2,1,0:T(8,128)(2,1)S(1)}, u32[]{:S(2)}, u32[]{:S(2)}) %all-to-all-start) | async-done | bytes 196640 | tf_op jit(solution)/shard_map/all_to_all | solution.py:262
  49.4 6.1 %shard_map.164 = bf16[32,24,128]{2,1,0:T(8,128)(2,1)S(1)} custom-call(s32[12]{0:T(128)S(1)} %dynamic_slice.3.pair_ref, f32[16,1024]{1,0:T(8,128)S(1)} %get-tuple-element.14.table_ref, f32[16,1024]{1,0:T(8,128)S(1)} %get-tuple-element.13.shifted_ref, bf16[12,769,128]{2,1,0:T(8,128)(2,1)S(1)} %copy-done.1, bf16[32,24,128]{2,1,0:T(8,128)(2,1)S(1)} %all-to-all-done.in_ref), custom_call_target="tpu_custom_call" | custom-call | tf_op jit(solution)/shard_map/pallas_call | solution.py:191
  55.5 0.0 copy-start.10
  55.6 0.0 copy-start.5
  55.6 11.4 %all_to_all.18 = bf16[32,24,128]{2,1,0:T(8,128)(2,1)S(1)} all-to-all(bf16[32,24,128]{2,1,0:T(8,128)(2,1)S(1)} %shard_map.164), channel_id=1, replica_groups=mesh['lat'=8,'lev'=4] {'lat','lev'}, dimensions={0} | all-to-all | bytes 393216 | tf_op jit(solution)/shard_map/all_to_all | solution.py:268
  67.0 0.5 fusion.15
  67.4 0.0 copy-start.9
  67.5 0.0 copy-start.6
  67.5 0.2 fusion.37
  67.7 0.2 fusion.40
  68.0 0.4 fusion.34
  68.4 0.1 copy-done.9
  68.5 0.3 convolution_add_fusion.1
  68.7 0.4 copy-done.6
  69.2 0.4 convolution_add_fusion
  69.6 0.0 copy-done.12
  69.7 0.2 add_convert_fusion.1
  69.9 0.8 %pad_maximum_fusion = bf16[3,1,16,5120]{3,2,1,0:T(8,128)(2,1)} fusion(bf16[3,1,16,1280]{3,2,1,0:T(8,128)(2,1)S(1)} %bitcast.59, bf16[3,1,16,1280]{3,2,1,0:T(8,128)(2,1)S(1)} %bitcast.58, bf16[3,1,16,1280]{3,2,1,0:T(8,128)(2,1)S(1)} %bitcast.60, bf16[3,1,16,1280]{3,2,1,0:T(8,128)(2,1)S(1)} %bitcast.57), kind=kLoop, calls=%fused_computation.27 | loop fusion | flops 1966080 | bytes 983040 | tf_op jit(solution)/shard_map/concatenate | solution.py:288
  (27 shorter events, 0.1 us)
Async XLA Ops:
  0.0 20.7 %copy-start = (bf16[3,1,16,5120]{3,2,1,0:T(8,128)(2,1)S(1)}, bf16[3,1,16,5120]{3,2,1,0:T(8,128)(2,1)}, u32[]{:S(2)}) copy-start(bf16[3,1,16,5120]{3,2,1,0:T(8,128)(2,1)} %param.17) | copy-start | bytes 1474564
  0.0 7.1 %copy-start.14 = (s32[384]{0:T(512)S(1)}, s32[384]{0:T(512)}, u32[]{:S(2)}) copy-start(s32[384]{0:T(512)} %param.20) | copy-start | bytes 4612
  0.0 20.7 %copy-start.2 = (bf16[4,1,16,5120]{3,2,1,0:T(8,128)(2,1)S(1)}, bf16[4,1,16,5120]{3,2,1,0:T(8,128)(2,1)}, u32[]{:S(2)}) copy-start(bf16[4,1,16,5120]{3,2,1,0:T(8,128)(2,1)} %param.19) | copy-start | bytes 1966084
  0.0 20.7 %copy-start.3 = (s32[1,16,5120]{2,1,0:T(8,128)S(1)}, s32[1,16,5120]{2,1,0:T(8,128)}, u32[]{:S(2)}) copy-start(s32[1,16,5120]{2,1,0:T(8,128)} %param.18) | copy-start | bytes 983044
  1.6 19.1 %collective-permute-start = (bf16[9,4,5120]{2,1,0:T(4,128)(2,1)S(1)}, bf16[9,4,5120]{2,1,0:T(4,128)(2,1)S(1)}, u32[]{:S(2)}, u32[]{:S(2)}) collective-permute-start(bf16[9,4,5120]{2,1,0:T(4,128)(2,1)S(1)} %reshape_squeeze.6), channel_id=1, source_target_pairs={{0,4},{4,8},{8,12},{12,16},{16,20},{20,24},{24,28},{1,5},{5,9},{9,... | collective-permute-start | bytes 1105928 | tf_op jit(solution)/shard_map/ppermute | solution.py:232
  5.8 14.9 %collective-permute-start.1 = (bf16[9,4,5120]{2,1,0:T(4,128)(2,1)S(1)}, bf16[9,4,5120]{2,1,0:T(4,128)(2,1)S(1)}, u32[]{:S(2)}, u32[]{:S(2)}) collective-permute-start(bf16[9,4,5120]{2,1,0:T(4,128)(2,1)S(1)} %reshape_squeeze.7), channel_id=1, source_target_pairs={{4,0},{8,4},{12,8},{16,12},{20,16},{24,20},{28,24},{5,1},{9,5},{13... | collective-permute-start | bytes 1105928 | tf_op jit(solution)/shard_map/ppermute | solution.py:233
  20.8 5.9 %copy-start.8 = (bf16[2,192,1280]{2,1,0:T(8,128)(2,1)S(1)}, bf16[2,192,1280]{2,1,0:T(8,128)(2,1)}, u32[]{:S(2)}) copy-start(bf16[2,192,1280]{2,1,0:T(8,128)(2,1)} %constant.47.clone) | copy-start | bytes 2949124
  20.8 6.4 %copy-start.7 = (bf16[2,192,1280]{2,1,0:T(8,128)(2,1)S(1)}, bf16[2,192,1280]{2,1,0:T(8,128)(2,1)}, u32[]{:S(2)}) copy-start(bf16[2,192,1280]{2,1,0:T(8,128)(2,1)} %constant.46.clone) | copy-start | bytes 2949124
  26.5 2.1 %copy-start.4 = (bf16[2,384,2560]{2,1,0:T(8,128)(2,1)S(1)}, bf16[2,384,2560]{2,1,0:T(8,128)(2,1)}, u32[]{:S(2)}) copy-start(bf16[2,384,2560]{2,1,0:T(8,128)(2,1)} %constant.48.clone) | copy-start | bytes 11796484
  27.6 2.4 %copy-start.15 = (s32[768]{0:T(1024)S(1)}, s32[768]{0:T(1024)}, u32[]{:S(2)}) copy-start(s32[768]{0:T(1024)} %constant.65) | copy-start | bytes 9220
  29.9 10.4 %copy-start.13 = (f32[768,4,4]{0,2,1:T(4,128)S(1)}, f32[768,4,4]{0,2,1:T(4,128)}, u32[]{:S(2)}) copy-start(f32[768,4,4]{0,2,1:T(4,128)} %param.22) | copy-start | bytes 147460
  29.9 19.6 %copy-start.1 = (bf16[12,769,128]{2,1,0:T(8,128)(2,1)S(1)}, bf16[12,769,128]{2,1,0:T(8,128)(2,1)}, u32[]{:S(2)}) copy-start(bf16[12,769,128]{2,1,0:T(8,128)(2,1)} %leg_ref.1) | copy-start | bytes 7087108
  31.2 35.8 %copy-start.16 = (bf16[768]{0:T(1024)(128)(2,1)S(1)}, bf16[768]{0:T(1024)(128)(2,1)}, u32[]{:S(2)}) copy-start(bf16[768]{0:T(1024)(128)(2,1)} %constant.104) | copy-start | bytes 4612
  32.1 17.3 %all-to-all-start = ((bf16[32,24,128]{2,1,0:T(8,128)(2,1)}), bf16[32,24,128]{2,1,0:T(8,128)(2,1)S(1)}, u32[]{:S(2)}, u32[]{:S(2)}) async-start(bf16[32,24,128]{2,1,0:T(8,128)(2,1)} %bitcast.14), calls=%async_computation | async-start | bytes 393216 | tf_op jit(solution)/shard_map/all_to_all | solution.py:262
  49.4 18.0 %copy-start.11 = (bf16[192,1280]{1,0:T(8,128)(2,1)S(1)}, bf16[192,1280]{1,0:T(8,128)(2,1)}, u32[]{:S(2)}) copy-start(bf16[192,1280]{1,0:T(8,128)(2,1)} %constant.53.clone) | copy-start | bytes 1474564
  55.5 12.2 %copy-start.10 = (bf16[192,1280]{1,0:T(8,128)(2,1)S(1)}, bf16[192,1280]{1,0:T(8,128)(2,1)}, u32[]{:S(2)}) copy-start(bf16[192,1280]{1,0:T(8,128)(2,1)} %constant.51.clone) | copy-start | bytes 1474564
  55.6 12.4 %copy-start.5 = (bf16[384,2560]{1,0:T(8,128)(2,1)S(1)}, bf16[384,2560]{1,0:T(8,128)(2,1)}, u32[]{:S(2)}) copy-start(bf16[384,2560]{1,0:T(8,128)(2,1)} %constant.55.clone) | copy-start | bytes 5898244
  67.4 1.0 %copy-start.9 = (bf16[192,1280]{1,0:T(8,128)(2,1)S(1)}, bf16[192,1280]{1,0:T(8,128)(2,1)}, u32[]{:S(2)}) copy-start(bf16[192,1280]{1,0:T(8,128)(2,1)} %constant.54.clone) | copy-start | bytes 1474564
  67.5 1.7 %copy-start.6 = (bf16[384,2560]{1,0:T(8,128)(2,1)S(1)}, bf16[384,2560]{1,0:T(8,128)(2,1)}, u32[]{:S(2)}) copy-start(bf16[384,2560]{1,0:T(8,128)(2,1)} %constant.56.clone) | copy-start | bytes 5898244
  68.5 1.2 %copy-start.12 = (bf16[192,1280]{1,0:T(8,128)(2,1)S(1)}, bf16[192,1280]{1,0:T(8,128)(2,1)}, u32[]{:S(2)}) copy-start(bf16[192,1280]{1,0:T(8,128)(2,1)} %constant.52.clone) | copy-start | bytes 1474564
